TPU v7x, 32 devices: a whole 2x2x4 slice. The times are simulated.
32 devices in a mesh: dp: 16 (over z, y, x), tensor: 2 (over core).
Axes of the slice: x: 2, y: 2, z: 4, core: 2. Of those that a mesh axis runs over, the one named last changes fastest.
Arguments:
- inputs: bfloat16 [32, 1024, 768], P('dp'), may hold values from -6 to 6
- segments: int32 [32, 1024], P('dp'), may hold values from 0 to 1, as said below
- token_marks: int32 [32, 1024], P('dp'), may hold values from 0 to 1, as said below
- cotangent: bfloat16 [32, 1024, 768], P('dp', 'tensor'), may hold values from -6 to 6
- heads_weight: float32 [3, 768, 768], P(None, 'dp', 'tensor')
- merge_weight: float32 [768, 768], P('tensor', 'dp')
- expand_weight: float32 [768, 3072], P('dp', 'tensor')
- reduce_weight: float32 [3072, 768], P('tensor', 'dp')
- norm_params: float32 [4, 768], P(None, ('dp', 'tensor'))
- first_heads: float32 [3, 768, 768], P(None, 'dp', 'tensor')
- first_merge: float32 [768, 768], P('tensor', 'dp')
- first_expand: float32 [768, 3072], P('dp', 'tensor')
- first_reduce: float32 [3072, 768], P('tensor', 'dp')
- first_norm: float32 [4, 768], P(None, ('dp', 'tensor')), may hold values from -4 to 4
- second_heads: float32 [3, 768, 768], P(None, 'dp', 'tensor'), may hold values from 0.01 to 1
- second_merge: float32 [768, 768], P('tensor', 'dp'), may hold values from 0.01 to 1
- second_expand: float32 [768, 3072], P('dp', 'tensor'), may hold values from 0.01 to 1
- second_reduce: float32 [3072, 768], P('tensor', 'dp'), may hold values from 0.01 to 1
- second_norm: float32 [4, 768], P(None, ('dp', 'tensor')), may hold values from 0.01 to 1
- step_count: int32 [], replicated, may hold values from 1 to 99
Outputs:
- layer_output: bfloat16 [32, 1024, 768], P('dp', 'tensor')
- input_grad: float32 [32, 1024, 768], P('dp', 'tensor')
- grad_heads: float32 [3, 768, 768], P(None, 'dp', 'tensor')
- grad_merge: float32 [768, 768], P('tensor', 'dp')
- grad_expand: float32 [768, 3072], P('dp', 'tensor')
- grad_reduce: float32 [3072, 768], P('tensor', 'dp')
- grad_norm: float32 [4, 768], P(None, ('dp', 'tensor'))
- next_first_heads: float32 [3, 768, 768], P(None, 'dp', 'tensor')
- next_first_merge: float32 [768, 768], P('tensor', 'dp')
- next_first_expand: float32 [768, 3072], P('dp', 'tensor')
- next_first_reduce: float32 [3072, 768], P('tensor', 'dp')
- next_first_norm: float32 [4, 768], P(None, ('dp', 'tensor'))
- next_second_heads: float32 [3, 768, 768], P(None, 'dp', 'tensor')
- next_second_merge: float32 [768, 768], P('tensor', 'dp')
- next_second_expand: float32 [768, 3072], P('dp', 'tensor')
- next_second_reduce: float32 [3072, 768], P('tensor', 'dp')
- next_second_norm: float32 [4, 768], P(None, ('dp', 'tensor'))
- next_heads_weight: float32 [3, 768, 768], P(None, 'dp', 'tensor')
- next_merge_weight: float32 [768, 768], P('tensor', 'dp')
- next_expand_weight: float32 [768, 3072], P('dp', 'tensor')
- next_reduce_weight: float32 [3072, 768], P('tensor', 'dp')
- next_norm_params: float32 [4, 768], P(None, ('dp', 'tensor'))
- trust_ratios: float32 [10], replicated
Inputs may be any that keep to these rules, and one draw needn't show every extreme that they name: `segments`: each row holds segment 0, its first 256 to 511 tokens, then segment 1 up to the row's end. `token_marks`: in each row one to 78 positions are 1, in runs of one to three; some row holds exactly 78 of them, all among its first 512 tokens.
All inputs are finite; a program needn't handle non-finite values.
Results may differ from a plain program's by a relative error of at most 0.018.
The roundings to bfloat16 on the way count: a program that leaves them out, or rounds other values in their place, can miss the bound.
Values may be sent and summed in bfloat16 or wider, within the bound.
No kernel may reach another device: no remote copies, remote signals or barrier semaphores. Data moves between devices by JAX's collectives and lax.ppermute only.
A program may use at most 192 MiB of HBM per device.

v0:
```python
import jax
import jax.numpy as jnp
from jax import lax
from jax.sharding import PartitionSpec as P

D = 768
HEAD = 64
SEQ = 1024


NORM_EPS = 1e-12
BETA_ONE = 0.9
BETA_TWO = 0.999
ADAM_EPS = 1e-06
DECAY = 0.01
RATE = 0.25
MASKED = -1000000000.0


def layer_norm_parts(values):
    average = jnp.mean(values, axis=-1, keepdims=True)
    centered = values - average
    spread = jnp.mean(centered * centered, axis=-1, keepdims=True)
    inverse = lax.rsqrt(spread + NORM_EPS)
    return (centered * inverse, inverse)


def norm_back(values, norm_gain, grad_out):
    normed, inverse = layer_norm_parts(values)
    scaled = grad_out * norm_gain
    grad_in = inverse * (
        scaled
        - jnp.mean(scaled, axis=-1, keepdims=True)
        - normed * jnp.mean(scaled * normed, axis=-1, keepdims=True)
    )
    return (grad_in, grad_out * normed)


def gelu_tanh(values):
    return (
        0.5
        * values
        * (1.0 + jnp.tanh(0.7978845608028654 * (values + 0.044715 * values * values * values)))
    )


def squares(heads_part, merge_part, expand_part, reduce_part, norm_part):
    return jnp.concatenate(
        [
            jnp.sum(heads_part * heads_part, axis=(1, 2)),
            jnp.sum(merge_part * merge_part)[None],
            jnp.sum(expand_part * expand_part)[None],
            jnp.sum(reduce_part * reduce_part)[None],
            jnp.sum(norm_part * norm_part, axis=1),
        ]
    )


def moments(weight, gradient, first, second, decay, corr_one, corr_two):
    next_first = BETA_ONE * first + (1.0 - BETA_ONE) * gradient
    next_second = BETA_TWO * second + (1.0 - BETA_TWO) * gradient * gradient
    update = next_first / corr_one / (jnp.sqrt(next_second / corr_two) + ADAM_EPS) + decay * weight
    return (next_first, next_second, update)


def shards(
    inputs,
    segments,
    token_marks,
    cotangent,
    heads_weight,
    merge_weight,
    expand_weight,
    reduce_weight,
    norm_params,
    first_heads,
    first_merge,
    first_expand,
    first_reduce,
    first_norm,
    second_heads,
    second_merge,
    second_expand,
    second_reduce,
    second_norm,
    step_count,
):
    tensor_size = lax.axis_size("tensor")
    member = lax.axis_index("tensor")
    rows_here = inputs.shape[0]
    half_seq = SEQ // tensor_size
    tokens = rows_here * SEQ
    local_width = heads_weight.shape[2]
    local_heads = local_width // HEAD
    score_scale = HEAD ** (-0.5)
    heads_full, merge_full, expand_full, reduce_full = (
        lax.all_gather(heads_weight.astype(jnp.bfloat16), "dp", axis=1, tiled=True),
        lax.all_gather(merge_weight.astype(jnp.bfloat16), "dp", axis=1, tiled=True),
        lax.all_gather(expand_weight.astype(jnp.bfloat16), "dp", axis=0, tiled=True),
        lax.all_gather(reduce_weight.astype(jnp.bfloat16), "dp", axis=1, tiled=True),
    )
    norms_full = lax.all_gather(norm_params, ("dp", "tensor"), axis=1, tiled=True)
    flat_in = inputs.reshape(tokens, D)
    own_in = lax.dynamic_slice_in_dim(inputs, member * half_seq, half_seq, 1).astype(jnp.float32)
    projected = jnp.einsum(
        "td,kde->kte", flat_in, heads_full, preferred_element_type=jnp.float32
    ).astype(jnp.bfloat16)
    proj_rows = projected.reshape(3, rows_here, SEQ, local_width)
    same_doc = segments[:, :, None] == segments[:, None, :]

    def attend_row(packed):
        queries, keys_row, values_row, same_row = packed
        query_heads = queries.reshape(SEQ, local_heads, HEAD)
        key_heads = keys_row.reshape(SEQ, local_heads, HEAD)
        value_heads = values_row.reshape(SEQ, local_heads, HEAD)
        scores = (
            jnp.einsum("qhd,khd->hqk", query_heads, key_heads, preferred_element_type=jnp.float32)
            * score_scale
        )
        masked = jnp.where(same_row[None], scores, MASKED)
        row_top = jnp.max(masked, axis=-1, keepdims=True)
        exp_scores = jnp.exp(masked - row_top)
        row_total = jnp.sum(exp_scores, axis=-1, keepdims=True)
        weights = (exp_scores / row_total).astype(jnp.bfloat16)
        context_row = jnp.einsum(
            "hqk,khd->qhd", weights, value_heads, preferred_element_type=jnp.float32
        )
        return (
            context_row.reshape(SEQ, local_width).astype(jnp.bfloat16),
            (row_top + jnp.log(row_total))[..., 0],
        )

    context, log_total = lax.map(attend_row, (proj_rows[0], proj_rows[1], proj_rows[2], same_doc))
    flat_context = context.reshape(tokens, local_width)
    merged_part = jnp.dot(flat_context, merge_full, preferred_element_type=jnp.float32).reshape(
        rows_here, SEQ, D
    )
    merged = lax.psum_scatter(merged_part, "tensor", scatter_dimension=1, tiled=True)
    attended = own_in + merged
    normed_one, unused_one = layer_norm_parts(attended)
    hidden_in = normed_one * norms_full[0] + norms_full[1]
    hidden_rows = lax.all_gather(hidden_in.astype(jnp.bfloat16), "tensor", axis=1, tiled=True)
    hidden_low = hidden_rows.reshape(tokens, D)
    ffn_inner = jnp.dot(hidden_low, expand_full, preferred_element_type=jnp.float32)
    hidden = gelu_tanh(ffn_inner).astype(jnp.bfloat16)
    reduced_part = jnp.dot(hidden, reduce_full, preferred_element_type=jnp.float32).reshape(
        rows_here, SEQ, D
    )
    reduced = lax.psum_scatter(
        reduced_part.astype(jnp.bfloat16), "tensor", scatter_dimension=1, tiled=True
    ).astype(jnp.float32)
    joined = hidden_in + reduced
    normed_two, unused_two = layer_norm_parts(joined)
    layer_output = (normed_two * norms_full[2] + norms_full[3]).astype(jnp.bfloat16)
    own_marks = lax.dynamic_slice_in_dim(token_marks, member * half_seq, half_seq, 1)
    seed_grad = cotangent.astype(jnp.float32) * own_marks.astype(jnp.float32)[..., None]
    shift_two = jnp.sum(seed_grad, axis=(0, 1))
    grad_joined, gain_two_terms = norm_back(joined, norms_full[2], seed_grad)
    gain_two = jnp.sum(gain_two_terms, axis=(0, 1))
    joined_low = lax.all_gather(
        grad_joined.astype(jnp.bfloat16), "tensor", axis=1, tiled=True
    ).reshape(tokens, D)
    grad_reduce_local = jnp.einsum(
        "tf,td->fd", hidden, joined_low, preferred_element_type=jnp.float32
    )
    back_hidden = jnp.einsum(
        "td,fd->tf", joined_low, reduce_full, preferred_element_type=jnp.float32
    )
    grad_inner = jax.vjp(gelu_tanh, ffn_inner)[1](back_hidden)[0].astype(jnp.bfloat16)
    grad_expand_local = jnp.einsum(
        "td,tf->df", hidden_low, grad_inner, preferred_element_type=jnp.float32
    )
    entry_part = jnp.einsum(
        "tf,df->td", grad_inner, expand_full, preferred_element_type=jnp.float32
    ).reshape(rows_here, SEQ, D)
    entry_grad = lax.psum_scatter(
        entry_part.astype(jnp.bfloat16), "tensor", scatter_dimension=1, tiled=True
    ).astype(jnp.float32)
    grad_hidden_in = entry_grad + grad_joined
    grad_attended, gain_one_terms = norm_back(attended, norms_full[0], grad_hidden_in)
    gain_one = jnp.sum(gain_one_terms, axis=(0, 1))
    shift_one = jnp.sum(grad_hidden_in, axis=(0, 1))
    attended_low = lax.all_gather(
        grad_attended.astype(jnp.bfloat16), "tensor", axis=1, tiled=True
    ).reshape(tokens, D)
    grad_merge_local = jnp.einsum(
        "te,td->ed", flat_context, attended_low, preferred_element_type=jnp.float32
    )
    grad_context = jnp.einsum(
        "td,ed->te", attended_low, merge_full, preferred_element_type=jnp.float32
    ).astype(jnp.bfloat16)
    grad_context = grad_context.reshape(rows_here, SEQ, local_width)

    def attend_back(packed):
        queries, keys_row, values_row, same_row, logs_row, grads_row = packed
        query_heads = queries.reshape(SEQ, local_heads, HEAD)
        key_heads = keys_row.reshape(SEQ, local_heads, HEAD)
        value_heads = values_row.reshape(SEQ, local_heads, HEAD)
        grad_heads_row = grads_row.reshape(SEQ, local_heads, HEAD)
        scores = (
            jnp.einsum("qhd,khd->hqk", query_heads, key_heads, preferred_element_type=jnp.float32)
            * score_scale
        )
        masked = jnp.where(same_row[None], scores, MASKED)
        probabilities = jnp.exp(masked - logs_row[..., None])
        weights = probabilities.astype(jnp.bfloat16)
        grad_probs = jnp.einsum(
            "qhd,khd->hqk", grad_heads_row, value_heads, preferred_element_type=jnp.float32
        )
        row_delta = jnp.sum(probabilities * grad_probs, axis=-1, keepdims=True)
        grad_scores = (probabilities * (grad_probs - row_delta)).astype(jnp.bfloat16)
        grad_query = (
            jnp.einsum("hqk,khd->qhd", grad_scores, key_heads, preferred_element_type=jnp.float32)
            * score_scale
        )
        grad_key = (
            jnp.einsum("hqk,qhd->khd", grad_scores, query_heads, preferred_element_type=jnp.float32)
            * score_scale
        )
        grad_value = jnp.einsum(
            "hqk,qhd->khd", weights, grad_heads_row, preferred_element_type=jnp.float32
        )
        return (
            grad_query.reshape(SEQ, local_width).astype(jnp.bfloat16),
            grad_key.reshape(SEQ, local_width).astype(jnp.bfloat16),
            grad_value.reshape(SEQ, local_width).astype(jnp.bfloat16),
        )

    grad_query_all, grad_key_all, grad_value_all = lax.map(
        attend_back, (proj_rows[0], proj_rows[1], proj_rows[2], same_doc, log_total, grad_context)
    )
    grad_flat = jnp.stack([grad_query_all, grad_key_all, grad_value_all]).reshape(
        3, tokens, local_width
    )
    input_part = jnp.einsum(
        "kte,kde->td", grad_flat, heads_full, preferred_element_type=jnp.float32
    ).reshape(rows_here, SEQ, D)
    grad_heads_local = jnp.einsum(
        "td,kte->kde", flat_in, grad_flat, preferred_element_type=jnp.float32
    )
    input_summed = lax.psum_scatter(
        input_part.astype(jnp.bfloat16), "tensor", scatter_dimension=1, tiled=True
    ).astype(jnp.float32)
    input_grad = input_summed + grad_attended
    part_heads, part_merge, part_expand, part_reduce = (
        lax.psum_scatter(grad_heads_local, "dp", scatter_dimension=1, tiled=True),
        lax.psum_scatter(grad_merge_local, "dp", scatter_dimension=1, tiled=True),
        lax.psum_scatter(grad_expand_local, "dp", scatter_dimension=0, tiled=True),
        lax.psum_scatter(grad_reduce_local, "dp", scatter_dimension=1, tiled=True),
    )
    norm_terms = jnp.stack([gain_one, shift_one, gain_two, shift_two])
    part_norm = lax.psum_scatter(norm_terms, ("dp", "tensor"), scatter_dimension=1, tiled=True)
    steps_float = step_count.astype(jnp.float32)
    corr_one = 1.0 - BETA_ONE**steps_float
    corr_two = 1.0 - BETA_TWO**steps_float
    first_h, second_h, update_h = moments(
        heads_weight, part_heads, first_heads, second_heads, DECAY, corr_one, corr_two
    )
    first_m, second_m, update_m = moments(
        merge_weight, part_merge, first_merge, second_merge, DECAY, corr_one, corr_two
    )
    first_e, second_e, update_e = moments(
        expand_weight, part_expand, first_expand, second_expand, DECAY, corr_one, corr_two
    )
    first_r, second_r, update_r = moments(
        reduce_weight, part_reduce, first_reduce, second_reduce, DECAY, corr_one, corr_two
    )
    first_n, second_n, update_n = moments(
        norm_params, part_norm, first_norm, second_norm, 0.0, corr_one, corr_two
    )
    update_squares = squares(update_h, update_m, update_e, update_r, update_n)
    weight_total, update_total = lax.psum(
        (
            squares(heads_weight, merge_weight, expand_weight, reduce_weight, norm_params),
            update_squares,
        ),
        ("dp", "tensor"),
    )
    trust_ratios = jnp.sqrt(weight_total) / jnp.sqrt(update_total + 1e-12)
    next_heads = heads_weight - RATE * trust_ratios[0:3, None, None] * update_h
    next_merge = merge_weight - RATE * trust_ratios[3] * update_m
    next_expand = expand_weight - RATE * trust_ratios[4] * update_e
    next_reduce = reduce_weight - RATE * trust_ratios[5] * update_r
    next_norm = norm_params - RATE * trust_ratios[6:10, None] * update_n
    return (
        layer_output,
        input_grad,
        part_heads,
        part_merge,
        part_expand,
        part_reduce,
        part_norm,
        first_h,
        first_m,
        first_e,
        first_r,
        first_n,
        second_h,
        second_m,
        second_e,
        second_r,
        second_n,
        next_heads,
        next_merge,
        next_expand,
        next_reduce,
        next_norm,
        trust_ratios,
    )


def solution(mesh):
    return jax.shard_map(
        shards,
        mesh=mesh,
        in_specs=(
            P("dp", None, None),
            P("dp", None),
            P("dp", None),
            P("dp", "tensor", None),
            P(None, "dp", "tensor"),
            P("tensor", "dp"),
            P("dp", "tensor"),
            P("tensor", "dp"),
            P(None, ("dp", "tensor")),
            P(None, "dp", "tensor"),
            P("tensor", "dp"),
            P("dp", "tensor"),
            P("tensor", "dp"),
            P(None, ("dp", "tensor")),
            P(None, "dp", "tensor"),
            P("tensor", "dp"),
            P("dp", "tensor"),
            P("tensor", "dp"),
            P(None, ("dp", "tensor")),
            P(),
        ),
        out_specs=(
            P("dp", "tensor", None),
            P("dp", "tensor", None),
            P(None, "dp", "tensor"),
            P("tensor", "dp"),
            P("dp", "tensor"),
            P("tensor", "dp"),
            P(None, ("dp", "tensor")),
            P(None, "dp", "tensor"),
            P("tensor", "dp"),
            P("dp", "tensor"),
            P("tensor", "dp"),
            P(None, ("dp", "tensor")),
            P(None, "dp", "tensor"),
            P("tensor", "dp"),
            P("dp", "tensor"),
            P("tensor", "dp"),
            P(None, ("dp", "tensor")),
            P(None, "dp", "tensor"),
            P("tensor", "dp"),
            P("dp", "tensor"),
            P("tensor", "dp"),
            P(None, ("dp", "tensor")),
            P(),
        ),
        check_vma=False,
    )
```

profile of v0, /device:TPU:0, one launch (start us, length us, event | category | flops | bytes accessed | tf_op | source)
XLA Modules:
  0.0 1118.2 jit_solution(10182150056892135386)
XLA Ops:
  11.1 49.1 %all_gather.25 = bf16[384,768]{0,1:T(8,128)(2,1)} all-gather(bf16[384,48]{0,1:T(8,128)(2,1)S(1)} %get-tuple-element.374), channel_id=1, replica_groups=mesh['dp'=16,'tensor'=2] {'dp'}, dimensions={1}, use_global_device_ids=true | all-gather | bytes 626688 | tf_op jit(solution)/shard_map/all_gather | solution.py:98
  62.3 12.3 %all-gather.8.cloned.1.call-done = bf16[3,768,384]{2,1,0:T(8,128)(2,1)} async-done(((bf16[3,48,384]{2,1,0:T(8,128)(2,1)}), bf16[3,768,384]{2,1,0:T(8,128)(2,1)}) %all-gather.8.cloned.1.call-update) | async-done | bytes 1769488 | tf_op jit(solution)/shard_map/all_gather | solution.py:97
  74.6 6.3 convert_bitcast_fusion
  83.3 3.8 squeeze.31
  90.2 3.8 squeeze.30
  105.2 76.3 %while.26 = (s32[]{:T(128)}, bf16[2,1024,384]{1,2,0:T(8,128)(2,1)}, f32[2,6,1024]{2,1,0:T(8,128)S(1)}, bf16[2,1024,384]{1,2,0:T(8,128)(2,1)}, pred[2,1024,1024]{...) while((s32[]{:T(128)}, bf16[2,1024,384]{1,2,0:T(8,128)(2,1)}, ...), condition=%wide.region_3.4_spmd, body=%wide.region_0.3_spmd.sunk | while | flops 1686497280 | bytes 102981800 | solution.py:133
  108.2 10.6 fusion.113
  118.9 11.2 %fusion.114 = f32[6,1024]{1,0:T(8,128)S(1)} fusion(f32[6,1024,1024]{1,2,0:T(8,128)} %get-tuple-element.487, f32[6,1024]{1,0:T(8,128)S(1)} %get-tuple-element.488, pred[1024,1024]{0,1:T(8,128)(4,1)S(1)} %dynamic-slice_bitcast_fusion.6), kind=kLoop, calls=%fused_computation.4.clone.1 | loop fusion | flops 25159680 | bytes 26263552 | tf_op jit(solution)/shard_map/while/body/eval_jaxpr/reduce_sum | solution.py:123
  130.1 12.2 %fusion.115 = bf16[6,64,1024]{2,1,0:T(8,128)(2,1)S(1)} fusion(bf16[1024,6,64]{0,2,1:T(8,128)(2,1)S(1)} %bitcast.190, f32[6,1024,1024]{1,2,0:T(8,128)} %get-tuple-element.487, f32[6,1024]{1,0:T(8,128)S(1)} %fusion.114, f32[6,1024]{1,0:T(8,128)S(1)} %get-tuple-element.488, pred[1024,1024]{0,1:T(8,128)(4,1)S(1)} %dynamic-slice_bitcast_fusion.6), kind=kOutput, calls=%fused_computation.7.clone.1 | convolution fusion | flops 837156864 | bytes 27836416 | tf_op jit(solution)/shard_map/while/body/eval_jaxpr/hqk,khd->qhd/dot_general | solution.py:125
  146.3 10.6 fusion.113
  156.9 11.2 %fusion.114 = f32[6,1024]{1,0:T(8,128)S(1)} fusion(f32[6,1024,1024]{1,2,0:T(8,128)} %get-tuple-element.487, f32[6,1024]{1,0:T(8,128)S(1)} %get-tuple-element.488, pred[1024,1024]{0,1:T(8,128)(4,1)S(1)} %dynamic-slice_bitcast_fusion.6), kind=kLoop, calls=%fused_computation.4.clone.1 | loop fusion | flops 25159680 | bytes 26263552 | tf_op jit(solution)/shard_map/while/body/eval_jaxpr/reduce_sum | solution.py:123
  168.1 12.2 %fusion.115 = bf16[6,64,1024]{2,1,0:T(8,128)(2,1)S(1)} fusion(bf16[1024,6,64]{0,2,1:T(8,128)(2,1)S(1)} %bitcast.190, f32[6,1024,1024]{1,2,0:T(8,128)} %get-tuple-element.487, f32[6,1024]{1,0:T(8,128)S(1)} %fusion.114, f32[6,1024]{1,0:T(8,128)S(1)} %get-tuple-element.488, pred[1024,1024]{0,1:T(8,128)(4,1)S(1)} %dynamic-slice_bitcast_fusion.6), kind=kOutput, calls=%fused_computation.7.clone.1 | convolution fusion | flops 837156864 | bytes 27836416 | tf_op jit(solution)/shard_map/while/body/eval_jaxpr/hqk,khd->qhd/dot_general | solution.py:125
  181.5 6.7 fusion.39
  190.5 39.6 %all-gather = f32[32,24,4]{1,2,0:T(4,128)S(1)} all-gather(f32[1,24,4]{1,2,0:T(4,128)S(1)} %bitcast.204), channel_id=1, replica_groups=mesh['dp'=16,'tensor'=2] {'dp','tensor'}, dimensions={0}, use_global_device_ids=true | all-gather | bytes 12672 | tf_op jit(solution)/shard_map/all_gather | solution.py:102
  236.8 32.2 %all-gather.12.cloned.1.call-done = bf16[768,1536]{1,0:T(8,128)(2,1)} async-done(((bf16[48,1536]{1,0:T(8,128)(2,1)}), bf16[768,1536]{1,0:T(8,128)(2,1)}) %all-gather.12.cloned.1.call-update) | async-done | bytes 2359312 | tf_op jit(solution)/shard_map/all_gather | solution.py:99
  269.0 13.0 %all-gather.10.cloned.1.call-done = bf16[2,1024,768]{2,1,0:T(8,128)(2,1)} async-done(((bf16[2,512,768]{2,1,0:T(8,128)(2,1)}), bf16[2,1024,768]{2,1,0:T(8,128)(2,1)}) %all-gather.10.cloned.1.call-update) | async-done | bytes 3145744 | tf_op jit(solution)/shard_map/all_gather | solution.py:142
  282.0 13.8 %multiply_convert_fusion.3 = (bf16[2048,1536]{1,0:T(8,128)(2,1)}, f32[2048,1536]{1,0:T(8,128)}) fusion(bf16[2048,768]{1,0:T(8,128)(2,1)} %bitcast.205, bf16[768,1536]{1,0:T(8,128)(2,1)} %all-gather.12.cloned.1.call-done), kind=kOutput, calls=%fused_computation.45 | convolution fusion | flops 4860149760 | bytes 24379392 | tf_op jit(solution)/shard_map/dot_general | solution.py:144
  295.8 53.3 %all-gather.14.cloned.1.call-done = bf16[1536,768]{0,1:T(8,128)(2,1)} async-done(((bf16[1536,48]{0,1:T(8,128)(2,1)}), bf16[1536,768]{0,1:T(8,128)(2,1)}) %all-gather.14.cloned.1.call-update) | async-done | bytes 2359312 | tf_op jit(solution)/shard_map/all_gather | solution.py:100
  349.1 9.0 convolution_convert_fusion.1
  358.8 9.2 reduce-scatter.11.cloned.1.call-done
  377.4 13.4 %all-gather.16.cloned.1.call-done = bf16[2,1024,768]{2,1,0:T(8,128)(2,1)} async-done(((bf16[2,512,768]{2,1,0:T(8,128)(2,1)}), bf16[2,1024,768]{2,1,0:T(8,128)(2,1)}) %all-gather.16.cloned.1.call-update) | async-done | bytes 3145744 | tf_op jit(solution)/shard_map/all_gather | solution.py:160
  390.8 17.1 %fusion.18 = bf16[2048,1536]{1,0:T(8,128)(2,1)S(1)} fusion(f32[2048,1536]{1,0:T(8,128)} %get-tuple-element.380, bf16[2048,768]{1,0:T(8,128)(2,1)} %bitcast.207, bf16[1536,768]{0,1:T(8,128)(2,1)} %all-gather.14.cloned.1.call-done), kind=kOutput, calls=%fused_computation.42 | convolution fusion | flops 4907335680 | bytes 24379392 | tf_op jit(solution)/shard_map/td,fd->tf/dot_general | solution.py:166
  407.9 6.5 convolution_convert_fusion
  414.5 12.2 %reduce-scatter.13.cloned.1.call-done = bf16[2,512,768]{2,1,0:T(8,128)(2,1)} async-done(((bf16[2,1024,768]{2,1,0:T(8,128)(2,1)}), bf16[2,512,768]{2,1,0:T(8,128)(2,1)}) %reduce-scatter.13.cloned.1.call-update) | async-done | bytes 1572880 | tf_op jit(solution)/shard_map/reduce_scatter | solution.py:176
  426.7 6.7 multiply_reduce_fusion.2
  436.9 9.8 fusion.58
  449.1 9.5 fusion.59
  459.7 5.0 convolution_convert_fusion.2
  471.9 155.2 %while.27 = (s32[]{:T(128)}, bf16[2,1024,384]{1,2,0:T(8,128)(2,1)}, bf16[2,1024,384]{1,2,0:T(8,128)(2,1)}, bf16[2,1024,384]{1,2,0:T(8,128)(2,1)}, bf16[2,1024,38...) while((s32[]{:T(128)}, bf16[2,1024,384]{1,2,0:T(8,128)(2,1)}, ...), condition=%wide.region_17.18_spmd, body=%wide.region_15.17_spmd.sunk | while | flops 4122863616 | bytes 268083696 | solution.py:229
  480.9 10.4 fusion.126
  491.3 12.7 %fusion.127 = bf16[6,64,1024]{2,1,0:T(8,128)(2,1)} fusion(bf16[1024,6,64]{0,2,1:T(8,128)(2,1)S(1)} %bitcast.189, f32[6,1024,1024]{1,2,0:T(8,128)} %fusion.126, f32[6,1024]{1,0:T(8,128)S(1)} %dynamic-slice_bitcast_fusion.7, pred[1024,1024]{0,1:T(8,128)(4,1)S(1)} %dynamic-slice_bitcast_fusion.8), kind=kOutput, calls=%fused_computation.24.clone.1 | convolution fusion | flops 830865408 | bytes 27811840 | tf_op jit(solution)/shard_map/while/body/eval_jaxpr/hqk,qhd->khd/dot_general | solution.py:220
  504.0 17.3 %multiply_reduce_fusion.19 = (f32[6,1024]{1,0:T(8,128)S(1)}, f32[6,1024,1024]{1,2,0:T(8,128)}) fusion(f32[6,1024,1024]{1,2,0:T(8,128)} %fusion.126, f32[6,1024]{1,0:T(8,128)S(1)} %dynamic-slice_bitcast_fusion.7, pred[1024,1024]{0,1:T(8,128)(4,1)S(1)} %dynamic-slice_bitcast_fusion.8, bf16[1024,6,64]{0,2,1:T(8,128)(2,1)} %bitcast.188, ...), kind=kOutput, calls=%fused_computation.16.clone.1 | convolution fusion | flops 836757504 | bytes 53002240 | tf_op jit(solution)/shard_map/while/body/eval_jaxpr/qhd,khd->hqk/dot_general | solution.py:207
  521.3 17.4 %multiply_convert_fusion.7 = bf16[6,1024,1024]{1,2,0:T(8,128)(2,1)S(1)} fusion(f32[6,1024,1024]{1,2,0:T(8,128)} %get-tuple-element.499, f32[6,1024,1024]{1,2,0:T(8,128)} %fusion.126, f32[6,1024]{1,0:T(8,128)S(1)} %get-tuple-element.500, f32[6,1024]{1,0:T(8,128)S(1)} %dynamic-slice_bitcast_fusion.7, pred[1024,1024]{0,1:T(8,128)(4,1)S(1)} %dynamic-slice_bitcast_fusion.8), kind=kLoop, calls=%fused_computation.15.clone.1 | loop fusion | flops 37748736 | bytes 64012288 | tf_op jit(solution)/shard_map/while/body/eval_jaxpr/convert_element_type | solution.py:211
  538.7 6.0 multiply_convert_fusion.9
  558.3 10.2 fusion.126
  568.5 12.8 %fusion.127 = bf16[6,64,1024]{2,1,0:T(8,128)(2,1)} fusion(bf16[1024,6,64]{0,2,1:T(8,128)(2,1)S(1)} %bitcast.189, f32[6,1024,1024]{1,2,0:T(8,128)} %fusion.126, f32[6,1024]{1,0:T(8,128)S(1)} %dynamic-slice_bitcast_fusion.7, pred[1024,1024]{0,1:T(8,128)(4,1)S(1)} %dynamic-slice_bitcast_fusion.8), kind=kOutput, calls=%fused_computation.24.clone.1 | convolution fusion | flops 830865408 | bytes 27811840 | tf_op jit(solution)/shard_map/while/body/eval_jaxpr/hqk,qhd->khd/dot_general | solution.py:220
  581.3 17.1 %multiply_reduce_fusion.19 = (f32[6,1024]{1,0:T(8,128)S(1)}, f32[6,1024,1024]{1,2,0:T(8,128)}) fusion(f32[6,1024,1024]{1,2,0:T(8,128)} %fusion.126, f32[6,1024]{1,0:T(8,128)S(1)} %dynamic-slice_bitcast_fusion.7, pred[1024,1024]{0,1:T(8,128)(4,1)S(1)} %dynamic-slice_bitcast_fusion.8, bf16[1024,6,64]{0,2,1:T(8,128)(2,1)} %bitcast.188, ...), kind=kOutput, calls=%fused_computation.16.clone.1 | convolution fusion | flops 836757504 | bytes 53002240 | tf_op jit(solution)/shard_map/while/body/eval_jaxpr/qhd,khd->hqk/dot_general | solution.py:207
  598.4 17.4 %multiply_convert_fusion.7 = bf16[6,1024,1024]{1,2,0:T(8,128)(2,1)S(1)} fusion(f32[6,1024,1024]{1,2,0:T(8,128)} %get-tuple-element.499, f32[6,1024,1024]{1,2,0:T(8,128)} %fusion.126, f32[6,1024]{1,0:T(8,128)S(1)} %get-tuple-element.500, f32[6,1024]{1,0:T(8,128)S(1)} %dynamic-slice_bitcast_fusion.7, pred[1024,1024]{0,1:T(8,128)(4,1)S(1)} %dynamic-slice_bitcast_fusion.8), kind=kLoop, calls=%fused_computation.15.clone.1 | loop fusion | flops 37748736 | bytes 64012288 | tf_op jit(solution)/shard_map/while/body/eval_jaxpr/convert_element_type | solution.py:211
  615.8 6.0 multiply_convert_fusion.9
  627.0 6.7 fusion.32
  633.8 4.1 copy.135
  647.6 5.6 bitcast_convert_fusion
  655.6 40.9 %all-reduce.1 = f32[4,768]{1,0:T(4,128)S(1)} all-reduce(f32[4,768]{1,0:T(4,128)S(1)} %pad_maximum_fusion.1), channel_id=10, replica_groups=mesh['dp'=16,'tensor'=2] {'dp','tensor'}, use_global_device_ids=true, to_apply=%region_27.28.clone | all-reduce | flops 3072 | bytes 24576
  702.0 35.4 %reduce-scatter.21.cloned.1.call-done = f32[1536,48]{0,1:T(8,128)} async-done(((f32[1536,768]{0,1:T(8,128)}), f32[1536,48]{0,1:T(8,128)}) %reduce-scatter.21.cloned.1.call-update) | async-done | bytes 294928 | tf_op jit(solution)/shard_map/reduce_scatter | solution.py:249
  739.9 126.1 %reduce-scatter.17.cloned.1.call-done = f32[384,48]{0,1:T(8,128)} async-done(((f32[384,768]{0,1:T(8,128)}), f32[384,48]{0,1:T(8,128)}) %reduce-scatter.17.cloned.1.call-update) | async-done | bytes 73744 | tf_op jit(solution)/shard_map/reduce_scatter | solution.py:247
  868.2 183.3 %all-reduce.5.cloned.1.call-done = f32[3,768,384]{2,0,1:T(4,128)} async-done(((f32[3,768,384]{2,0,1:T(4,128)}), f32[3,768,384]{2,0,1:T(4,128)}) %all-reduce.5.cloned.1.call-update) | async-done | bytes 3538960
  1057.1 39.5 %all-reduce.2 = (f32[10]{0:T(128)S(1)}, f32[10]{0:T(128)}) all-reduce(f32[10]{0:T(128)} %concatenate.8, f32[10]{0:T(128)S(1)} %concatenate.7), channel_id=1, replica_groups=mesh['dp'=16,'tensor'=2] {'dp','tensor'}, use_global_device_ids=true, to_apply=%region_39.40 | all-reduce | flops 20 | bytes 160 | tf_op jit(solution)/shard_map/psum | solution.py:272
  1107.4 4.1 convert_add_fusion
  (272 shorter events, 125.8 us)
Async XLA Ops:
  7.2 67.4 %all-gather.8.cloned.1.call-start = ((), (), s32[]{:S(2)}) async-start(), calls=%async_computation.7 | async-start | bytes 1880064 | tf_op jit(solution)/shard_map/all_gather | solution.py:97
  9.5 220.8 %reduce-scatter.9.cloned.1.call-start = ((), (), s32[]{:S(2)}) async-start(), calls=%async_computation.8 | async-start | bytes 9437184 | tf_op jit(solution)/shard_map/reduce_scatter | solution.py:138
  105.2 76.4 %copy-start.27 = (bf16[384,768]{0,1:T(8,128)(2,1)S(1)}, bf16[384,768]{0,1:T(8,128)(2,1)}, u32[]{:S(2)}) copy-start(bf16[384,768]{0,1:T(8,128)(2,1)} %all_gather.25) | copy-start | bytes 1769476
  130.1 12.2 %copy-start.19 = (bf16[2,1024,384]{1,2,0:T(8,128)(2,1)S(1)}, bf16[2,1024,384]{1,2,0:T(8,128)(2,1)}, u32[]{:S(2)}) copy-start(bf16[2,1024,384]{1,2,0:T(8,128)(2,1)} %get-tuple-element.512) | copy-start | bytes 4718596 | tf_op jit(solution)/shard_map/while
  168.1 12.2 %copy-start.19 = (bf16[2,1024,384]{1,2,0:T(8,128)(2,1)S(1)}, bf16[2,1024,384]{1,2,0:T(8,128)(2,1)}, u32[]{:S(2)}) copy-start(bf16[2,1024,384]{1,2,0:T(8,128)(2,1)} %get-tuple-element.512) | copy-start | bytes 4718596 | tf_op jit(solution)/shard_map/while
  181.5 6.7 copy-start.7
  188.2 80.8 %all-gather.12.cloned.1.call-start = ((), (), s32[]{:S(2)}) async-start(), calls=%async_computation.10 | async-start | bytes 2506752 | tf_op jit(solution)/shard_map/all_gather | solution.py:99
  190.5 91.5 %all-gather.10.cloned.1.call-start = ((), (), s32[]{:S(2)}) async-start(), calls=%async_computation.9 | async-start | bytes 4718592 | tf_op jit(solution)/shard_map/all_gather | solution.py:142
  230.2 203.2 %copy-start.36 = (f32[768]{0:T(1024)}, f32[768]{0:T(1024)S(1)}, u32[]{:S(2)}) copy-start(f32[768]{0:T(1024)S(1)} %get-tuple-element.291) | copy-start | bytes 9220
  233.2 200.3 %copy-start.1 = (f32[2,512,768]{2,1,0:T(8,128)}, f32[2,512,768]{2,1,0:T(8,128)S(1)}, u32[]{:S(2)}) copy-start(f32[2,512,768]{2,1,0:T(8,128)S(1)} %get-tuple-element.354) | copy-start | bytes 9437188
  233.2 200.3 %copy-start.34 = (f32[2,512]{1,0:T(2,128)}, f32[2,512]{1,0:T(2,128)S(1)}, u32[]{:S(2)}) copy-start(f32[2,512]{1,0:T(2,128)S(1)} %broadcast_multiply_fusion.5) | copy-start | bytes 12292
  233.7 199.8 %copy-start.38 = (f32[2,512]{1,0:T(2,128)}, f32[2,512]{1,0:T(2,128)S(1)}, u32[]{:S(2)}) copy-start(f32[2,512]{1,0:T(2,128)S(1)} %add_rsqrt_fusion.1) | copy-start | bytes 12292
  235.4 113.7 %all-gather.14.cloned.1.call-start = ((), (), s32[]{:S(2)}) async-start(), calls=%async_computation.11 | async-start | bytes 2506752 | tf_op jit(solution)/shard_map/all_gather | solution.py:100
  236.8 131.3 %reduce-scatter.11.cloned.1.call-start = ((), (), s32[]{:S(2)}) async-start(), calls=%async_computation.12 | async-start | bytes 4718592 | tf_op jit(solution)/shard_map/reduce_scatter | solution.py:149
  358.2 32.6 %all-gather.16.cloned.1.call-start = ((), (), s32[]{:S(2)}) async-start(), calls=%async_computation.13 | async-start | bytes 4718592 | tf_op jit(solution)/shard_map/all_gather | solution.py:160
  377.4 49.3 %reduce-scatter.13.cloned.1.call-start = ((), (), s32[]{:S(2)}) async-start(), calls=%async_computation.14 | async-start | bytes 4718592 | tf_op jit(solution)/shard_map/reduce_scatter | solution.py:176
  390.8 17.1 %copy-start.57 = (bf16[768,1536]{1,0:T(8,128)(2,1)S(1)}, bf16[768,1536]{1,0:T(8,128)(2,1)}, u32[]{:S(2)}) copy-start(bf16[768,1536]{1,0:T(8,128)(2,1)} %all-gather.12.cloned.1.call-done) | copy-start | bytes 7077892
  407.9 6.5 copy-start.60
  414.5 44.3 %all-gather.18.cloned.1.call-start = ((), (), s32[]{:S(2)}) async-start(), calls=%async_computation.15 | async-start | bytes 4718592 | tf_op jit(solution)/shard_map/all_gather | solution.py:183
  436.9 262.5 %reduce-scatter.19.cloned.1.call-start = ((), (), s32[]{:S(2)}) async-start(), calls=%async_computation.18 | async-start | bytes 5013504 | tf_op jit(solution)/shard_map/reduce_scatter | solution.py:248
  446.8 290.5 %reduce-scatter.21.cloned.1.call-start = ((), (), s32[]{:S(2)}) async-start(), calls=%async_computation.19 | async-start | bytes 5013504 | tf_op jit(solution)/shard_map/reduce_scatter | solution.py:249
  458.7 407.3 %reduce-scatter.17.cloned.1.call-start = ((), (), s32[]{:S(2)}) async-start(), calls=%async_computation.17 | async-start | bytes 1253376 | tf_op jit(solution)/shard_map/reduce_scatter | solution.py:247
  459.7 5.0 copy-start.56
  467.8 583.7 %all-reduce.5.cloned.1.call-start = ((), (), s32[]{:S(2)}) async-start(), calls=%async_computation.20 | async-start | bytes 9437184
  480.9 10.4 copy-start.6
  491.3 12.7 %copy-start.5 = (bf16[1,1024,384]{1,2,0:T(8,128)(2,1)S(1)}, bf16[1,1024,384]{1,2,0:T(8,128)(2,1)}, u32[]{:S(2)}) copy-start(bf16[1,1024,384]{1,2,0:T(8,128)(2,1)} %constant_dynamic-slice_fusion.21) | copy-start | bytes 2359300 | tf_op jit(solution)/shard_map/while
  558.3 10.2 copy-start.6
  568.5 12.8 %copy-start.5 = (bf16[1,1024,384]{1,2,0:T(8,128)(2,1)S(1)}, bf16[1,1024,384]{1,2,0:T(8,128)(2,1)}, u32[]{:S(2)}) copy-start(bf16[1,1024,384]{1,2,0:T(8,128)(2,1)} %constant_dynamic-slice_fusion.21) | copy-start | bytes 2359300 | tf_op jit(solution)/shard_map/while
  637.9 5.7 copy-start.16
  637.9 469.4 %reduce-scatter.15.cloned.1.call-start = ((), (), s32[]{:S(2)}) async-start(), calls=%async_computation.16 | async-start | bytes 4718592 | tf_op jit(solution)/shard_map/reduce_scatter | solution.py:241
  653.2 43.3 %copy-start.45 = (f32[4,24]{1,0:T(4,128)S(1)}, f32[4,24]{1,0:T(4,128)}, u32[]{:S(2)}) copy-start(f32[4,24]{1,0:T(4,128)} %param.32) | copy-start | bytes 1156
  653.2 43.2 %copy-start.52 = (f32[4,24]{1,0:T(4,128)S(1)}, f32[4,24]{1,0:T(4,128)}, u32[]{:S(2)}) copy-start(f32[4,24]{1,0:T(4,128)} %param.42) | copy-start | bytes 1156
  653.3 43.2 %copy-start.53 = (f32[4,24]{1,0:T(4,128)S(1)}, f32[4,24]{1,0:T(4,128)}, u32[]{:S(2)}) copy-start(f32[4,24]{1,0:T(4,128)} %param.37) | copy-start | bytes 1156
  653.3 44.0 %copy-start.51 = (f32[3]{0:T(128)S(1)}, f32[3]{0:T(128)}, u32[]{:S(2)}) copy-start(f32[3]{0:T(128)} %get-tuple-element.371) | copy-start | bytes 40
  653.3 46.1 %copy-start.26 = (f32[48,1536]{1,0:T(8,128)S(1)}, f32[48,1536]{1,0:T(8,128)}, u32[]{:S(2)}) copy-start(f32[48,1536]{1,0:T(8,128)} %param.30) | copy-start | bytes 884740
  653.3 46.1 %copy-start.30 = (f32[48,1536]{1,0:T(8,128)S(1)}, f32[48,1536]{1,0:T(8,128)}, u32[]{:S(2)}) copy-start(f32[48,1536]{1,0:T(8,128)} %param.40) | copy-start | bytes 884740
  653.3 46.1 %copy-start.31 = (f32[48,1536]{1,0:T(8,128)S(1)}, f32[48,1536]{1,0:T(8,128)}, u32[]{:S(2)}) copy-start(f32[48,1536]{1,0:T(8,128)} %param.35) | copy-start | bytes 884740
  653.3 84.0 %copy-start.24 = (f32[1536,48]{0,1:T(8,128)S(1)}, f32[1536,48]{0,1:T(8,128)}, u32[]{:S(2)}) copy-start(f32[1536,48]{0,1:T(8,128)} %param.31) | copy-start | bytes 884740
  653.3 84.0 %copy-start.32 = (f32[1536,48]{0,1:T(8,128)S(1)}, f32[1536,48]{0,1:T(8,128)}, u32[]{:S(2)}) copy-start(f32[1536,48]{0,1:T(8,128)} %param.41) | copy-start | bytes 884740
  653.3 84.0 %copy-start.33 = (f32[1536,48]{0,1:T(8,128)S(1)}, f32[1536,48]{0,1:T(8,128)}, u32[]{:S(2)}) copy-start(f32[1536,48]{0,1:T(8,128)} %param.36) | copy-start | bytes 884740
  653.4 212.6 %copy-start.29 = (f32[384,48]{0,1:T(8,128)S(1)}, f32[384,48]{0,1:T(8,128)}, u32[]{:S(2)}) copy-start(f32[384,48]{0,1:T(8,128)} %param.29) | copy-start | bytes 221188
  739.9 367.5 %copy-start.2 = (f32[2,512,768]{2,1,0:T(8,128)S(1)}, f32[2,512,768]{2,1,0:T(8,128)}, u32[]{:S(2)}) copy-start(f32[2,512,768]{2,1,0:T(8,128)} %copy-done.1) | copy-start | bytes 9437188
  739.9 367.5 %copy-start.35 = (f32[2,512]{1,0:T(2,128)S(1)}, f32[2,512]{1,0:T(2,128)}, u32[]{:S(2)}) copy-start(f32[2,512]{1,0:T(2,128)} %copy-done.34) | copy-start | bytes 12292
  739.9 367.5 %copy-start.37 = (f32[768]{0:T(1024)S(1)}, f32[768]{0:T(1024)}, u32[]{:S(2)}) copy-start(f32[768]{0:T(1024)} %copy-done.36) | copy-start | bytes 9220
  739.9 367.5 %copy-start.39 = (f32[2,512]{1,0:T(2,128)S(1)}, f32[2,512]{1,0:T(2,128)}, u32[]{:S(2)}) copy-start(f32[2,512]{1,0:T(2,128)} %copy-done.38) | copy-start | bytes 12292
  739.9 367.5 %copy-start.41 = (f32[2,512]{1,0:T(2,128)S(1)}, f32[2,512]{1,0:T(2,128)}, u32[]{:S(2)}) copy-start(f32[2,512]{1,0:T(2,128)} %copy-done.40) | copy-start | bytes 12292
  739.9 367.5 %copy-start.43 = (f32[2,512]{1,0:T(2,128)S(1)}, f32[2,512]{1,0:T(2,128)}, u32[]{:S(2)}) copy-start(f32[2,512]{1,0:T(2,128)} %copy-done.42) | copy-start | bytes 12292
  1097.3 14.2 %copy-start.50 = (f32[10]{0:T(128)}, f32[10]{0:T(128)S(1)}, u32[]{:S(2)}) copy-start(f32[10]{0:T(128)S(1)} %rsqrt_multiply_fusion) | copy-start | bytes 124
  (40 other events, 90.8 us)
Sparse Core Ops, SparseCore 0:
  11.3 63.3 all-gather.7
  188.3 13.2 reduce-scatter.8
  205.4 63.5 all-gather.11
  271.0 10.9 all-gather.9
  285.6 63.4 all-gather.13
  358.3 9.7 reduce-scatter.10
  377.5 13.2 all-gather.15
  414.6 12.0 reduce-scatter.12
  437.0 13.2 all-gather.17
  456.7 138.5 reduce-scatter.18
  601.1 136.1 reduce-scatter.20
  743.2 122.6 reduce-scatter.16
  872.6 178.7 all-reduce.4
  1054.1 9.9 reduce-scatter.14
where the time goes:
time: 1130 us; the launch traced here: 1120 us
  waiting for transfers between devices  490 us (43%)
  matrix products  242 us (21%)
  blocking collectives  169 us (15%)
  other arithmetic  112 us (10%)
  local copies, waits for them, and re-layouts  85.6 us (8%)
  between operations  18 us (2%)
    unnamed x15, waiting for transfers between devices  183 us
    reduce_scatter x1, waiting for transfers between devices, shards(): lax.psum_scatter(grad_merge_local, 'dp', scatter_dimension=1, tiled=True)  126 us
    all_gather x1, waiting for transfers between devices, shards(): lax.all_gather(reduce_weight.astype(jnp.bfloat16), 'dp', axis=1, tiled=True)  53.3 us
    all_gather x1, blocking collectives, shards(): lax.all_gather(merge_weight.astype(jnp.bfloat16), 'dp', axis=1, tiled=True)  49.1 us
    unnamed x1, blocking collectives  40.9 us
    all_gather x1, blocking collectives, shards(): lax.all_gather(norm_params, ('dp', 'tensor'), axis=1, tiled=True)  39.6 us
    psum x1, blocking collectives, shards(): lax.psum((squares(heads_weight, merge_weight, expand_weight, reduce_weigh...  39.5 us
    reduce_scatter x1, waiting for transfers between devices, shards(): lax.psum_scatter(grad_reduce_local, 'dp', scatter_dimension=1, tiled=True)  35.4 us
  transfers between devices with their start and end apart: 14, of which 10 were waited for; matrix products, arithmetic and copies ran while one was open for 23% of the time, Pallas kernels for 0%

commit v1 on v0

v1 whole, which is shorter than its diff:
```python
import functools

import jax
import jax.numpy as jnp
from jax import lax
from jax.experimental import pallas as pl
from jax.experimental.pallas import tpu as pltpu
from jax.sharding import PartitionSpec as P

D = 768
HEAD = 64
SEQ = 1024
FF = 3072
HALF = D // 2
FF_HALF = FF // 2
MARKED = 80
BLOCKS = 16
ROWS_OF = D // BLOCKS
NORM_COLS = 128
PAIRS = D // 128
MIB = 1 << 20

NORM_EPS = 1e-12
BETA_ONE = 0.9
BETA_TWO = 0.999
ADAM_EPS = 1e-06
DECAY = 0.01
RATE = 0.25
MASKED = -1000000000.0
SCALE = HEAD ** (-0.5)
GELU_A = 0.7978845608028654
GELU_B = 0.044715
ALL = ("dp", "tensor")
LOW = jnp.bfloat16
WIDE = jnp.float32


def dot(left, right):
    return jnp.dot(left, right, preferred_element_type=WIDE)


def dot_last(left, right):
    return lax.dot_general(left, right, (((1,), (1,)), ((), ())), preferred_element_type=WIDE)


def dot_first(left, right):
    return lax.dot_general(left, right, (((0,), (0,)), ((), ())), preferred_element_type=WIDE)


def layer_norm_parts(values):
    average = jnp.mean(values, axis=-1, keepdims=True)
    centered = values - average
    spread = jnp.mean(centered * centered, axis=-1, keepdims=True)
    inverse = lax.rsqrt(spread + NORM_EPS)
    return centered * inverse, inverse


def norm_back(normed, inverse, gain, grad_out):
    scaled = grad_out * gain
    return inverse * (
        scaled
        - jnp.mean(scaled, axis=-1, keepdims=True)
        - normed * jnp.mean(scaled * normed, axis=-1, keepdims=True)
    )


def gelu_tanh(values):
    return 0.5 * values * (1.0 + jnp.tanh(GELU_A * (values + GELU_B * values * values * values)))


def gelu_slope(values):
    square = values * values
    bent = jnp.tanh(GELU_A * (values + GELU_B * square * values))
    return 0.5 * (1.0 + bent) + 0.5 * values * (1.0 - bent * bent) * (
        GELU_A * (1.0 + 3.0 * GELU_B * square)
    )


def moments(weight, gradient, first, second, decay, corr_one, corr_two):
    next_first = BETA_ONE * first + (1.0 - BETA_ONE) * gradient
    next_second = BETA_TWO * second + (1.0 - BETA_TWO) * gradient * gradient
    update = next_first / corr_one / (jnp.sqrt(next_second / corr_two) + ADAM_EPS) + decay * weight
    return (next_first, next_second, update)


def squares(heads_part, merge_part, expand_part, reduce_part, norm_part):
    return jnp.concatenate(
        [
            jnp.sum(heads_part * heads_part, axis=(1, 2)),
            jnp.sum(merge_part * merge_part)[None],
            jnp.sum(expand_part * expand_part)[None],
            jnp.sum(reduce_part * reduce_part)[None],
            jnp.sum(norm_part * norm_part, axis=1),
        ]
    )


def weight_copies(info, pieces, columns, target, target_columns, sem, pick=None, both=True):
    member = info[0]
    width = columns[1] - columns[0]
    copies = []
    for half in range(2 if both else 1):
        if both:
            side = member if half == 0 else 1 - member
            start = pl.multiple_of(target_columns + side * width, 128)
        else:
            start = target_columns
        for place in range(BLOCKS):
            source = pieces[2 * half + place // 8]
            row = pl.multiple_of(info[1 + half * BLOCKS + place] * ROWS_OF, 16)
            if pick is None:
                from_ref = source.at[place % 8, :, pl.ds(columns[0], width)]
                to_ref = target.at[pl.ds(row, ROWS_OF), pl.ds(start, width)]
            else:
                from_ref = source.at[place % 8]
                to_ref = target.at[:, pl.ds(row, ROWS_OF), pl.ds(start, width)]
            copies.append(
                pltpu.make_async_copy(from_ref, to_ref, sem.at[half * BLOCKS + place])
            )
    return copies


def start_all(copies):
    for copy in copies:
        copy.start()


def wait_all(copies):
    for copy in copies:
        copy.wait()


def qkv_kernel(info, x_ref, a, b, c, d, out_ref, weight, sem):
    @pl.when(pl.program_id(0) == 0)
    def _():
        copies = weight_copies(info, (a, b, c, d), (0, HALF), weight, 0, sem, pick=True)
        start_all(copies)
        wait_all(copies)

    for kind in range(3):
        out_ref[:, kind * D : (kind + 1) * D] = dot(x_ref[...], weight[kind]).astype(LOW)


def lane_mask(rows, which):
    lanes = lax.broadcasted_iota(jnp.int32, (rows, 128), 1)
    return (lanes < HEAD) if which == 0 else (lanes >= HEAD)


def attend_kernel(q_ref, k_ref, v_ref, seg_row_ref, seg_col_ref, out_ref):
    seg_row = seg_row_ref[...]
    zero = jnp.float32(0)
    tiles = (
        (0, 0, 512, None),
        (256, 0, 1024, None),
        (512, 256, 1024, None),
        (768, 256, 1024, None),
    )
    for start, low, high, _unused in tiles:
        if start == 256:
            bias = jnp.where(seg_col_ref[256:512, :] == seg_row, zero, MASKED)
        else:
            bias = jnp.where(
                seg_row[:, low:high] == (0 if start == 0 else 1), zero, MASKED
            )
        queries = q_ref[start : start + 256, :] * jnp.asarray(SCALE, LOW)
        result = None
        for which in range(2):
            mask = lane_mask(256, which)
            own = jnp.where(mask, queries, jnp.zeros_like(queries))
            scores = dot_last(own, k_ref[low:high, :]) + bias
            top = jnp.max(scores, axis=-1, keepdims=True)
            exped = jnp.exp(scores - top)
            total = jnp.sum(exped, axis=-1, keepdims=True)
            weights = (exped * (1.0 / total)).astype(LOW)
            context = dot(weights, v_ref[low:high, :])
            result = context if which == 0 else jnp.where(mask, context, result)
        out_ref[start : start + 256, :] = result.astype(LOW)


def marked_one_kernel(
    info, sel_ref, x_ref, ctx_ref, norms, a, b, c, d,
    xm_ref, cm_ref, att_ref, y_ref, yb_ref, u_ref, h_ref,
    merge, expand, sem, sem_two,
):
    merge_copies = weight_copies(info, (a, b, c, d), (0, HALF), merge, 0, sem)
    expand_copies = weight_copies(info, (a, b, c, d), (HALF, HALF + FF_HALF), expand, 0, sem_two)
    start_all(merge_copies)
    start_all(expand_copies)
    chosen = sel_ref[...]
    x_marked = dot(chosen, x_ref[...])
    xm_ref[...] = x_marked.astype(LOW)
    c_marked = dot(chosen, ctx_ref[...]).astype(LOW)
    cm_ref[...] = c_marked
    wait_all(merge_copies)
    attended = x_marked + dot_last(c_marked, merge[...])
    att_ref[...] = attended
    normed, _unused = layer_norm_parts(attended)
    y = normed * norms[0:1, :] + norms[1:2, :]
    y_ref[...] = y
    low = y.astype(LOW)
    yb_ref[...] = low
    wait_all(expand_copies)

    @pl.loop(0, FF // 512)
    def _(step):
        columns = pl.ds(pl.multiple_of(step * 512, 512), 512)
        inner = dot(low, expand[:, columns])
        u_ref[:, columns] = inner
        h_ref[:, columns] = gelu_tanh(inner).astype(LOW)


def marked_two_kernel(
    info, sel_ref, cot_a, cot_b, norms, y_ref, h_ref, a, b, c, d,
    db_ref, dbb_ref, ng_ref, reduce_w, sem,
):
    copies = weight_copies(info, (a, b, c, d), (0, FF_HALF), reduce_w, 0, sem)
    start_all(copies)
    first = info[0] == 0
    half = SEQ // 2
    chosen = sel_ref[...]
    cot_low = jnp.where(first, cot_a[...], cot_b[...])
    cot_high = jnp.where(first, cot_b[...], cot_a[...])
    grad = dot(chosen[:, :half], cot_low) + dot(chosen[:, half:], cot_high)
    wait_all(copies)
    joined = y_ref[...] + dot_last(h_ref[...], reduce_w[...])
    normed, inverse = layer_norm_parts(joined)
    back = norm_back(normed, inverse, norms[2:3, :], grad)
    db_ref[...] = back
    dbb_ref[...] = back.astype(LOW)
    ng_ref[0:1, :] = jnp.sum(grad * normed, axis=0, keepdims=True)
    ng_ref[1:2, :] = jnp.sum(grad, axis=0, keepdims=True)


def marked_three_kernel(
    info, norms, db_ref, dbb_ref, u_ref, att_ref, a, b, c, d, e, f, g, h,
    da_ref, dab_ref, dc_ref, ng_ref, merge, expand, reduce_w, du, sem, sem_two, sem_three,
):
    reduce_copies = weight_copies(info, (e, f, g, h), (0, FF_HALF), reduce_w, 0, sem_three)
    expand_copies = weight_copies(info, (a, b, c, d), (HALF, HALF + FF_HALF), expand, 0, sem_two)
    merge_copies = weight_copies(info, (a, b, c, d), (0, HALF), merge, 0, sem)
    start_all(reduce_copies)
    start_all(expand_copies)
    start_all(merge_copies)
    low = dbb_ref[...]
    wait_all(reduce_copies)

    @pl.loop(0, FF // 512)
    def _(step):
        columns = pl.ds(pl.multiple_of(step * 512, 512), 512)
        du[:, columns] = (
            dot(low, reduce_w[:, columns]) * gelu_slope(u_ref[:, columns])
        ).astype(LOW)

    wait_all(expand_copies)
    grad_y = db_ref[...] + dot_last(du[...], expand[...])
    normed, inverse = layer_norm_parts(att_ref[...])
    grad_a = norm_back(normed, inverse, norms[0:1, :], grad_y)
    da_ref[...] = grad_a
    grad_low = grad_a.astype(LOW)
    dab_ref[...] = grad_low
    ng_ref[0:1, :] = jnp.sum(grad_y * normed, axis=0, keepdims=True)
    ng_ref[1:2, :] = jnp.sum(grad_y, axis=0, keepdims=True)
    wait_all(merge_copies)
    dc_ref[...] = dot(grad_low, merge[...]).astype(LOW)


def attend_back_kernel(
    sel_ref, q_ref, k_ref, v_ref, dc_ref, seg_row_ref, seg_mark_ref, dq_ref, dk_ref, dv_ref
):
    queries = dot(sel_ref[...], q_ref[...]).astype(LOW)
    keys, values, grads = k_ref[...], v_ref[...], dc_ref[...]
    same = seg_mark_ref[...] == seg_row_ref[...]
    none = jnp.zeros_like(queries)
    query_list, grad_list, weight_list, score_list, dq = [], [], [], [], None
    for which in range(2):
        mask = lane_mask(MARKED, which)
        own = jnp.where(mask, queries, none)
        own_grad = jnp.where(mask, grads, none)
        scores = dot_last(own * jnp.asarray(SCALE, LOW), keys)
        scores = jnp.where(same, scores, MASKED)
        top = jnp.max(scores, axis=-1, keepdims=True)
        exped = jnp.exp(scores - top)
        probs = exped * (1.0 / jnp.sum(exped, axis=-1, keepdims=True))
        grad_probs = dot_last(own_grad, values)
        delta = jnp.sum(probs * grad_probs, axis=-1, keepdims=True)
        grad_scores = (probs * (grad_probs - delta)).astype(LOW)
        part = dot(grad_scores, keys) * SCALE
        dq = part if which == 0 else jnp.where(mask, part, dq)
        query_list.append(own)
        grad_list.append(own_grad)
        weight_list.append(probs.astype(LOW))
        score_list.append(grad_scores)
    dq_ref[...] = dq.astype(LOW)
    dk_ref[...] = (
        dot_first(jnp.concatenate(score_list, 0), jnp.concatenate(query_list, 0)) * SCALE
    ).astype(LOW)
    dv_ref[...] = dot_first(
        jnp.concatenate(weight_list, 0), jnp.concatenate(grad_list, 0)
    ).astype(LOW)


def heads_grad_kernel(
    info, x_ref, dk_ref, dv_ref, xm_ref, dq_ref, cm_ref, dab_ref,
    keep_ref, send_ref, par_ref, total, sem,
):
    step = pl.program_id(0)
    half = lax.rem(step, 2)

    def put(kind, value):
        total[half, :, pl.ds(kind * HALF, HALF)] = value.astype(LOW)

    @pl.when(step < 2)
    def _():
        put(0, dot_first(xm_ref[...], dq_ref[...]))

    @pl.when((step >= 2) & (step < 4))
    def _():
        put(1, dot_first(x_ref[...], dk_ref[...]))

    @pl.when((step >= 4) & (step < 6))
    def _():
        put(2, dot_first(x_ref[...], dv_ref[...]))

    @pl.when(step >= 6)
    def _():
        put(3, dot_first(dab_ref[...], cm_ref[...]))

    @pl.when(step == 7)
    def _():
        member = info[0]
        copies = []
        for place in range(2 * BLOCKS):
            row = pl.multiple_of(info[1 + place] * ROWS_OF, 16)
            if place < BLOCKS:
                side, target = member, (keep_ref if place < 8 else send_ref).at[place % 8]
            else:
                side, target = 1 - member, par_ref.at[place - BLOCKS]
            copies.append(
                pltpu.make_async_copy(
                    total.at[side, pl.ds(row, ROWS_OF), :], target, sem.at[place]
                )
            )
        start_all(copies)
        wait_all(copies)


def ffn_grad_kernel(
    info, yb_ref, db_ref, ybc_ref, dbc_ref, a, b, c, d,
    out_ref, expand, reduce_w, hid, du, block, sem, sem_two,
):
    expand_copies = weight_copies(
        info, (a, b), (HALF, HALF + FF_HALF), expand, 0, sem, both=False
    )
    reduce_copies = weight_copies(info, (c, d), (0, FF_HALF), reduce_w, 0, sem_two, both=False)
    start_all(expand_copies)
    start_all(reduce_copies)
    wait_all(expand_copies)
    wait_all(reduce_copies)
    tokens = yb_ref.shape[0]

    @pl.loop(0, FF_HALF // 256)
    def _(step):
        columns = pl.ds(pl.multiple_of(step * 256, 256), 256)
        later = pl.ds(pl.multiple_of(FF_HALF + step * 256, 256), 256)
        inner = dot(yb_ref[...], expand[:, columns])
        hid[...] = gelu_tanh(inner).astype(LOW)
        du[...] = (dot(db_ref[...], reduce_w[:, columns]) * gelu_slope(inner)).astype(LOW)
        block[:, columns] = dot_first(ybc_ref[...], du[...]).astype(LOW)
        block[:, later] = dot_first(dbc_ref[...], hid[...]).astype(LOW)

    for place in range(4):
        row = pl.multiple_of(lax.rem(info[1 + 4 * place], 4) * ROWS_OF, 16)
        out_ref[place] = block[pl.ds(row, ROWS_OF), :]


def input_grad_kernel(
    info, dk_ref, dv_ref, sel_ref, da_ref, dq_ref, a, b, c, d, out_ref,
    weight, high, low, sem,
):
    @pl.when(pl.program_id(0) == 0)
    def _():
        copies = weight_copies(info, (a, b, c, d), (0, HALF), weight, 0, sem, pick=True)
        start_all(copies)
        wait_all(copies)
        extra = da_ref[...] + dot_last(dq_ref[...], weight[0])
        top = extra.astype(LOW)
        high[...] = top
        low[...] = (extra - top.astype(WIDE)).astype(LOW)

    chosen = sel_ref[...]
    out_ref[...] = (
        dot_last(dk_ref[...], weight[1])
        + dot_last(dv_ref[...], weight[2])
        + dot_first(chosen, high[...])
        + dot_first(chosen, low[...])
    )


def forward_kernel(
    info, x_ref, ctx_ref, norms, a, b, c, d, e, f, g, h, out_ref,
    merge, expand, reduce_w, sem, sem_two, sem_three,
):
    @pl.when(pl.program_id(0) == 0)
    def _():
        copies = (
            weight_copies(info, (a, b, c, d), (0, HALF), merge, 0, sem)
            + weight_copies(info, (a, b, c, d), (HALF, HALF + FF_HALF), expand, 0, sem_two)
            + weight_copies(info, (e, f, g, h), (0, FF_HALF), reduce_w, 0, sem_three)
        )
        start_all(copies)
        wait_all(copies)

    attended = x_ref[...].astype(WIDE) + dot_last(ctx_ref[...], merge[...])
    normed, _unused = layer_norm_parts(attended)
    y = normed * norms[0:1, :] + norms[1:2, :]
    low = y.astype(LOW)
    joined = y
    for step in range(FF // 768):
        columns = slice(step * 768, (step + 1) * 768)
        hidden = gelu_tanh(dot(low, expand[:, columns])).astype(LOW)
        joined = joined + dot_last(hidden, reduce_w[:, columns])
    normed_two, _unused_two = layer_norm_parts(joined)
    out_ref[...] = (normed_two * norms[2:3, :] + norms[3:4, :]).astype(LOW)


ANY = pl.BlockSpec(memory_space=pl.ANY)
SMEM = pl.BlockSpec(memory_space=pltpu.SMEM)
VMEM = pl.BlockSpec(memory_space=pltpu.VMEM)


def shape(dims, kind):
    return jax.ShapeDtypeStruct(dims, kind)


def params(mib):
    return pltpu.CompilerParams(vmem_limit_bytes=mib * MIB)


def cost(flops, moved, hard=0):
    return pl.CostEstimate(flops=int(flops), bytes_accessed=int(moved), transcendentals=int(hard))


def sems(count=2 * BLOCKS):
    return pltpu.SemaphoreType.DMA((count,))


def whole(dims):
    return pl.BlockSpec(dims, lambda *_: (0,) * len(dims))


def call_qkv(info, x, first):
    return pl.pallas_call(
        qkv_kernel,
        grid=(4,),
        in_specs=[SMEM, pl.BlockSpec((256, D), lambda i: (i, 0)), ANY, ANY, ANY, ANY],
        out_specs=pl.BlockSpec((256, 3 * D), lambda i: (i, 0)),
        out_shape=shape((SEQ, 3 * D), LOW),
        scratch_shapes=[pltpu.VMEM((3, D, D), LOW), sems()],
        compiler_params=params(32),
        cost_estimate=cost(2 * SEQ * D * 3 * D, 10e6),
        name="project",
    )(info, x, *first)


def call_attend(qkv, seg_row, seg_col):
    def at(base):
        return pl.BlockSpec((SEQ, 128), lambda i, base=base: (0, base + i))

    return pl.pallas_call(
        attend_kernel,
        grid=(PAIRS,),
        in_specs=[at(0), at(PAIRS), at(2 * PAIRS), whole((1, SEQ)), whole((SEQ, 1))],
        out_specs=at(0),
        out_shape=shape((SEQ, D), LOW),
        compiler_params=params(32),
        cost_estimate=cost(3 * SEQ * SEQ * 128 * 12, 6e6, 9e6),
        name="attend",
    )(qkv, qkv, qkv, seg_row, seg_col)


def call_marked_one(info, sel, x, context, norms, second):
    return pl.pallas_call(
        marked_one_kernel,
        in_specs=[SMEM, VMEM, VMEM, VMEM, VMEM, ANY, ANY, ANY, ANY],
        out_specs=[VMEM] * 7,
        out_shape=[
            shape((MARKED, D), LOW),
            shape((MARKED, D), LOW),
            shape((MARKED, D), WIDE),
            shape((MARKED, D), WIDE),
            shape((MARKED, D), LOW),
            shape((MARKED, FF), WIDE),
            shape((MARKED, FF), LOW),
        ],
        scratch_shapes=[pltpu.VMEM((D, D), LOW), pltpu.VMEM((D, FF), LOW), sems(), sems()],
        compiler_params=params(32),
        cost_estimate=cost(1.5e9, 12e6),
        name="marked_one",
    )(info, sel, x, context, norms, *second)


def call_marked_two(info, sel, cot_own, cot_other, norms, y, hidden, third):
    return pl.pallas_call(
        marked_two_kernel,
        in_specs=[SMEM, VMEM, VMEM, VMEM, VMEM, VMEM, VMEM, ANY, ANY, ANY, ANY],
        out_specs=[VMEM] * 3,
        out_shape=[
            shape((MARKED, D), WIDE),
            shape((MARKED, D), LOW),
            shape((2, D), WIDE),
        ],
        scratch_shapes=[pltpu.VMEM((D, FF), LOW), sems()],
        compiler_params=params(32),
        cost_estimate=cost(1e9, 8e6),
        name="marked_two",
    )(info, sel, cot_own, cot_other, norms, y, hidden, *third)


def call_marked_three(info, norms, grad_b, grad_b_low, inner, attended, second, third):
    return pl.pallas_call(
        marked_three_kernel,
        in_specs=[SMEM] + [VMEM] * 5 + [ANY] * 8,
        out_specs=[VMEM] * 4,
        out_shape=[
            shape((MARKED, D), WIDE),
            shape((MARKED, D), LOW),
            shape((MARKED, D), LOW),
            shape((2, D), WIDE),
        ],
        scratch_shapes=[
            pltpu.VMEM((D, D), LOW),
            pltpu.VMEM((D, FF), LOW),
            pltpu.VMEM((D, FF), LOW),
            pltpu.VMEM((MARKED, FF), LOW),
            sems(),
            sems(),
            sems(),
        ],
        compiler_params=params(32),
        cost_estimate=cost(1.5e9, 12e6),
        name="marked_three",
    )(info, norms, grad_b, grad_b_low, inner, attended, *second, *third)


def call_attend_back(sel, qkv, grad_context, seg_row, seg_mark):
    def at(base):
        return pl.BlockSpec((SEQ, 128), lambda i, base=base: (0, base + i))

    small = pl.BlockSpec((MARKED, 128), lambda i: (0, i))
    return pl.pallas_call(
        attend_back_kernel,
        grid=(PAIRS,),
        in_specs=[
            whole((MARKED, SEQ)),
            at(0),
            at(PAIRS),
            at(2 * PAIRS),
            small,
            whole((1, SEQ)),
            whole((MARKED, 1)),
        ],
        out_specs=[small, at(0), at(0)],
        out_shape=[shape((MARKED, D), LOW), shape((SEQ, D), LOW), shape((SEQ, D), LOW)],
        compiler_params=params(32),
        cost_estimate=cost(12 * 12 * MARKED * SEQ * 128, 8e6, 1e6),
        name="attend_back",
    )(sel, qkv, qkv, qkv, grad_context, seg_row, seg_mark)


def call_heads_grad(info, x, grad_k, grad_v, x_marked, grad_q, c_marked, grad_a_low):
    def part(rows):
        return pl.BlockSpec((rows, HALF), lambda i: (0, lax.rem(i, 2)))

    return pl.pallas_call(
        heads_grad_kernel,
        grid=(8,),
        in_specs=[
            SMEM,
            whole((SEQ, D)),
            part(SEQ),
            part(SEQ),
            whole((MARKED, D)),
            part(MARKED),
            part(MARKED),
            whole((MARKED, D)),
        ],
        out_specs=[ANY] * 3,
        out_shape=[
            shape((8, ROWS_OF, 4 * HALF), LOW),
            shape((8, ROWS_OF, 4 * HALF), LOW),
            shape((BLOCKS, ROWS_OF, 4 * HALF), LOW),
        ],
        scratch_shapes=[pltpu.VMEM((2, D, 4 * HALF), LOW), sems()],
        compiler_params=params(40),
        cost_estimate=cost(2 * SEQ * D * 2 * D, 12e6),
        name="heads_grad",
    )(info, x, grad_k, grad_v, x_marked, grad_q, c_marked, grad_a_low)


def call_ffn_grad(info, yb, db, yb_part, db_part, second, third):
    tokens = yb.shape[0]
    return pl.pallas_call(
        ffn_grad_kernel,
        in_specs=[SMEM] + [VMEM] * 4 + [ANY] * 4,
        out_specs=VMEM,
        out_shape=shape((4, ROWS_OF, FF), LOW),
        scratch_shapes=[
            pltpu.VMEM((D, FF_HALF), LOW),
            pltpu.VMEM((D, FF_HALF), LOW),
            pltpu.VMEM((tokens, 256), LOW),
            pltpu.VMEM((tokens, 256), LOW),
            pltpu.VMEM((4 * ROWS_OF, FF), LOW),
            sems(BLOCKS),
            sems(BLOCKS),
        ],
        compiler_params=params(32),
        cost_estimate=cost(5e9, 10e6),
        name="ffn_grad",
    )(info, yb, db, yb_part, db_part, second[0], second[1], third[0], third[1])


def call_input_grad(info, grad_k, grad_v, sel, grad_a, grad_q, first):
    tile = pl.BlockSpec((256, D), lambda i: (i, 0))
    return pl.pallas_call(
        input_grad_kernel,
        grid=(4,),
        in_specs=[
            SMEM,
            tile,
            tile,
            pl.BlockSpec((MARKED, 256), lambda i: (0, i)),
            whole((MARKED, D)),
            whole((MARKED, D)),
            ANY,
            ANY,
            ANY,
            ANY,
        ],
        out_specs=tile,
        out_shape=shape((SEQ, D), WIDE),
        scratch_shapes=[
            pltpu.VMEM((3, D, D), LOW),
            pltpu.VMEM((MARKED, D), LOW),
            pltpu.VMEM((MARKED, D), LOW),
            sems(),
        ],
        compiler_params=params(32),
        cost_estimate=cost(2 * SEQ * D * 2 * D, 10e6),
        name="input_grad",
    )(info, grad_k, grad_v, sel, grad_a, grad_q, *first)


def call_forward(info, x, context, norms, second, third):
    tile = pl.BlockSpec((256, D), lambda i: (i, 0))
    return pl.pallas_call(
        forward_kernel,
        grid=(4,),
        in_specs=[SMEM, tile, tile, whole((4, D))] + [ANY] * 8,
        out_specs=tile,
        out_shape=shape((SEQ, D), LOW),
        scratch_shapes=[
            pltpu.VMEM((D, D), LOW),
            pltpu.VMEM((D, FF), LOW),
            pltpu.VMEM((D, FF), LOW),
            sems(),
            sems(),
            sems(),
        ],
        compiler_params=params(48),
        cost_estimate=cost(2 * SEQ * D * (D + 2 * FF), 14e6),
        name="forward_rest",
    )(info, x, context, norms, *second, *third)


class Grid:
    def __init__(self, depth, rows, columns):
        self.depth, self.rows, self.columns = depth, rows, columns
        self.chips = depth * rows * columns

    def chip(self, z, y, x):
        return (z * self.rows + y) * self.columns + x

    def perm(self, where):
        pairs = []
        for z in range(self.depth):
            for y in range(self.rows):
                for x in range(self.columns):
                    for t in range(2):
                        z2, y2, x2, t2 = where(z, y, x, t)
                        pairs.append(
                            (self.chip(z, y, x) * 2 + t, self.chip(z2, y2, x2) * 2 + t2)
                        )
        return pairs

    def send(self, value, where):
        return lax.ppermute(value, ALL, self.perm(where))

    def along_z(self, value, step):
        return self.send(value, lambda z, y, x, t: (z ^ step, y, x, t))

    def inner(self, value):
        return self.send(value, lambda z, y, x, t: (z, y ^ (1 - t), x ^ t, t))

    def outer(self, value):
        return self.send(value, lambda z, y, x, t: (z, y ^ t, x ^ (1 - t), t))

    def gather_z(self, value):
        return jnp.concatenate([value] + [self.along_z(value, s) for s in range(1, self.depth)], 0)

    def gather(self, value):
        column = self.gather_z(value)
        eight = jnp.concatenate([column, self.inner(column)], 0)
        return eight, self.outer(eight)


def other_core(value):
    return lax.ppermute(value, "tensor", [(0, 1), (1, 0)])


def shards(
    fast,
    inputs,
    segments,
    token_marks,
    cotangent,
    heads_weight,
    merge_weight,
    expand_weight,
    reduce_weight,
    norm_params,
    first_heads,
    first_merge,
    first_expand,
    first_reduce,
    first_norm,
    second_heads,
    second_merge,
    second_expand,
    second_reduce,
    second_norm,
    step_count,
):
    member = lax.axis_index("tensor")
    here = lax.axis_index("dp")
    grid = Grid(4, 2, 2)
    half_seq = SEQ // 2
    shard_rows = heads_weight.shape[1]
    norm_width = norm_params.shape[1]

    if fast:
        z, y, x = here // 4, (here // 2) % 2, here % 2

        def places(core):
            place = jnp.arange(BLOCKS, dtype=jnp.int32)
            far, near, deep = place // 8, (place // 4) % 2, place % 4
            y_place = jnp.where(core == 0, near, far)
            x_place = jnp.where(core == 0, far, near)
            return (z ^ deep) * 4 + (y ^ y_place) * 2 + (x ^ x_place)

        info = jnp.concatenate([member[None], places(member), places(1 - member)])
    else:
        order = jnp.arange(BLOCKS, dtype=jnp.int32)
        info = jnp.concatenate([member[None], order, order])
    info = info.astype(jnp.int32)

    first_part = heads_weight.astype(LOW)
    merge_turned = merge_weight.astype(LOW).T
    second_list = [merge_turned, expand_weight.astype(LOW)]
    if fast:
        top = norm_params.astype(LOW)
        rest = norm_params - top.astype(WIDE)
        middle = rest.astype(LOW)
        last = (rest - middle.astype(WIDE)).astype(LOW)
        packed = jnp.concatenate([top, middle, last], 0)
        second_list.append(
            jnp.pad(packed, ((0, ROWS_OF - 12), (0, NORM_COLS - norm_width)))
        )
    second_part = jnp.concatenate(second_list, 1)
    third_part = reduce_weight.astype(LOW).T

    if fast:

        def pieces(part):
            eight, rest_eight = grid.gather(part[None])
            return eight, rest_eight, other_core(eight), other_core(rest_eight)

    else:

        def pieces(part):
            full = lax.all_gather(part, "dp", axis=part.ndim - 2, tiled=True)
            if part.ndim == 3:
                blocks = full.reshape(3, BLOCKS, ROWS_OF, HALF).transpose(1, 0, 2, 3)
            else:
                blocks = full.reshape(BLOCKS, ROWS_OF, part.shape[1])
            eight, rest_eight = blocks[:8], blocks[8:]
            return eight, rest_eight, other_core(eight), other_core(rest_eight)

    first_w = pieces(first_part)
    second_w = pieces(second_part)
    third_w = pieces(third_part)

    if fast:

        def norm_side(eight, rest_eight, table):
            both = jnp.concatenate(
                [v[:, :12, HALF + FF_HALF : HALF + FF_HALF + norm_width] for v in (eight, rest_eight)]
            ).astype(WIDE)
            summed = both[:, 0:4] + both[:, 4:8] + both[:, 8:12]
            place_of = jnp.sum(
                jnp.where(
                    table[None, :] == jnp.arange(BLOCKS)[:, None], jnp.arange(BLOCKS)[None, :], 0
                ),
                axis=1,
            )
            return summed[place_of]

        own_side = norm_side(second_w[0], second_w[1], info[1:17])
        other_side = norm_side(second_w[2], second_w[3], info[17:33])
        low_side = jnp.where(member == 0, own_side, other_side)
        high_side = jnp.where(member == 0, other_side, own_side)
        norms = jnp.stack([low_side, high_side], 1).transpose(2, 0, 1, 3).reshape(4, D)
    else:
        norms = lax.all_gather(norm_params, ALL, axis=1, tiled=True)

    x_row = lax.dynamic_index_in_dim(inputs, member, 0, keepdims=False)
    segment = lax.dynamic_index_in_dim(segments, member, 0, keepdims=False)
    marks = lax.dynamic_index_in_dim(token_marks, member, 0, keepdims=False)
    rank = jnp.cumsum(marks) - 1
    sel = (
        (rank[None, :] == jnp.arange(MARKED, dtype=jnp.int32)[:, None]) & (marks[None, :] == 1)
    ).astype(LOW)
    seg_row, seg_col = segment[None, :], segment[:, None]
    seg_mark = jnp.sum(
        jnp.where(sel > 0, segment[None, :], 0), axis=1, keepdims=True, dtype=jnp.int32
    )
    cot_own = lax.dynamic_index_in_dim(cotangent, member, 0, keepdims=False)
    cot_other = other_core(lax.dynamic_index_in_dim(cotangent, 1 - member, 0, keepdims=False))

    qkv = call_qkv(info, x_row, first_w)
    context = call_attend(qkv, seg_row, seg_col)
    x_marked, c_marked, attended, y_marked, yb, inner, hidden = call_marked_one(
        info, sel, x_row, context, norms, second_w
    )
    grad_b, dbb, norm_two = call_marked_two(
        info, sel, cot_own, cot_other, norms, y_marked, hidden, third_w
    )
    grad_a, dab, grad_context, norm_one = call_marked_three(
        info, norms, grad_b, dbb, inner, attended, second_w, third_w
    )
    grad_q, grad_k, grad_v = call_attend_back(sel, qkv, grad_context, seg_row, seg_mark)

    if fast:

        def shared(value):
            column = grid.gather_z(value)
            return jnp.concatenate([column, other_core(column)], 0)

        yb_all, db_all = shared(yb), shared(dbb)
        wide = D // 4
        yb_cols = lax.dynamic_slice_in_dim(yb_all, z * wide, wide, 1)
        db_cols = lax.dynamic_slice_in_dim(db_all, z * wide, wide, 1)
        four = call_ffn_grad(info, yb_all, db_all, yb_cols, db_cols, second_w, third_w)
        two = four[:2].astype(WIDE) + grid.outer(four[2:]).astype(WIDE)
        one = two[0] + grid.inner(two[1].astype(LOW)).astype(WIDE)
        part_expand, part_reduce = one[:, :FF_HALF], one[:, FF_HALF:].T
    else:
        yb_all = jnp.concatenate([yb, other_core(yb)], 0)
        db_all = jnp.concatenate([dbb, other_core(dbb)], 0)
        expand_half = jnp.concatenate(second_w[:2], 0).reshape(D, -1)[:, HALF : HALF + FF_HALF]
        reduce_half = jnp.concatenate(third_w[:2], 0).reshape(D, -1)
        inner_all = dot(yb_all, expand_half)
        back_all = (dot(db_all, reduce_half) * gelu_slope(inner_all)).astype(LOW)
        hidden_all = gelu_tanh(inner_all).astype(LOW)
        part_expand = lax.psum_scatter(
            dot_first(yb_all, back_all), "dp", scatter_dimension=0, tiled=True
        )
        part_reduce = lax.psum_scatter(
            dot_first(db_all, hidden_all), "dp", scatter_dimension=0, tiled=True
        ).T

    keep, give, other = call_heads_grad(
        info, x_row, grad_k, grad_v, x_marked, grad_q, c_marked, dab
    )
    came = other_core(other)
    if fast:
        eight = keep.astype(WIDE) + came[:8].astype(WIDE)
        eight_give = (give.astype(WIDE) + came[8:].astype(WIDE)).astype(LOW)
        eight = eight + grid.outer(eight_give).astype(WIDE)
        four_h = eight[:4] + grid.inner(eight[4:].astype(LOW)).astype(WIDE)
        low_four = four_h.astype(LOW)
        summed = four_h[0]
        for step in range(1, 4):
            summed = summed + grid.along_z(low_four[step], step).astype(WIDE)
    else:
        full = jnp.concatenate([keep, give], 0).astype(WIDE) + came.astype(WIDE)
        summed = lax.psum_scatter(
            full.reshape(D, 4 * HALF), "dp", scatter_dimension=0, tiled=True
        )
    part_heads = jnp.stack([summed[:, k * HALF : (k + 1) * HALF] for k in range(3)], 0)
    part_merge = summed[:, 3 * HALF :].T

    def halves(row):
        mine = lax.dynamic_slice_in_dim(row, member * half_seq, half_seq, 0)
        give_half = lax.dynamic_slice_in_dim(row, (1 - member) * half_seq, half_seq, 0)
        return mine, other_core(give_half.astype(LOW))

    def place_rows(mine, came_half):
        came_half = came_half.astype(mine.dtype)
        return jnp.where(
            member == 0, jnp.stack([mine, came_half]), jnp.stack([came_half, mine])
        )

    layer_output = place_rows(*halves(call_forward(info, x_row, context, norms, second_w, third_w)))
    input_grad = place_rows(
        *halves(call_input_grad(info, grad_k, grad_v, sel, grad_a, grad_q, first_w))
    )

    norm_terms = jnp.concatenate([norm_one, norm_two], 0)
    part_norm = lax.psum_scatter(norm_terms, ALL, scatter_dimension=1, tiled=True)

    steps_float = step_count.astype(WIDE)
    corr_one = 1.0 - BETA_ONE**steps_float
    corr_two = 1.0 - BETA_TWO**steps_float
    first_h, second_h, update_h = moments(
        heads_weight, part_heads, first_heads, second_heads, DECAY, corr_one, corr_two
    )
    first_m, second_m, update_m = moments(
        merge_weight, part_merge, first_merge, second_merge, DECAY, corr_one, corr_two
    )
    first_e, second_e, update_e = moments(
        expand_weight, part_expand, first_expand, second_expand, DECAY, corr_one, corr_two
    )
    first_r, second_r, update_r = moments(
        reduce_weight, part_reduce, first_reduce, second_reduce, DECAY, corr_one, corr_two
    )
    first_n, second_n, update_n = moments(
        norm_params, part_norm, first_norm, second_norm, 0.0, corr_one, corr_two
    )
    both = jnp.stack(
        [
            squares(heads_weight, merge_weight, expand_weight, reduce_weight, norm_params),
            squares(update_h, update_m, update_e, update_r, update_n),
        ]
    )
    if fast:
        both = both + other_core(both)
        both = (
            both
            + grid.send(both, lambda z, y, x, t: (z, y ^ 1, x, t))
            + grid.send(both, lambda z, y, x, t: (z, y, x ^ 1, t))
            + grid.send(both, lambda z, y, x, t: (z, y ^ 1, x ^ 1, t))
        )
        both = (both + grid.along_z(both, 1)) + (grid.along_z(both, 2) + grid.along_z(both, 3))
    else:
        both = lax.psum(both, ALL)
    trust_ratios = jnp.sqrt(both[0]) / jnp.sqrt(both[1] + 1e-12)
    next_heads = heads_weight - RATE * trust_ratios[0:3, None, None] * update_h
    next_merge = merge_weight - RATE * trust_ratios[3] * update_m
    next_expand = expand_weight - RATE * trust_ratios[4] * update_e
    next_reduce = reduce_weight - RATE * trust_ratios[5] * update_r
    next_norm = norm_params - RATE * trust_ratios[6:10, None] * update_n
    return (
        layer_output,
        input_grad,
        part_heads,
        part_merge,
        part_expand,
        part_reduce,
        part_norm,
        first_h,
        first_m,
        first_e,
        first_r,
        first_n,
        second_h,
        second_m,
        second_e,
        second_r,
        second_n,
        next_heads,
        next_merge,
        next_expand,
        next_reduce,
        next_norm,
        trust_ratios,
    )


def solution(mesh):
    fast = mesh.shape["dp"] == BLOCKS and mesh.shape["tensor"] == 2
    return jax.shard_map(
        functools.partial(shards, fast),
        mesh=mesh,
        in_specs=(
            P("dp", None, None),
            P("dp", None),
            P("dp", None),
            P("dp", "tensor", None),
            P(None, "dp", "tensor"),
            P("tensor", "dp"),
            P("dp", "tensor"),
            P("tensor", "dp"),
            P(None, ("dp", "tensor")),
            P(None, "dp", "tensor"),
            P("tensor", "dp"),
            P("dp", "tensor"),
            P("tensor", "dp"),
            P(None, ("dp", "tensor")),
            P(None, "dp", "tensor"),
            P("tensor", "dp"),
            P("dp", "tensor"),
            P("tensor", "dp"),
            P(None, ("dp", "tensor")),
            P(),
        ),
        out_specs=(
            P("dp", "tensor", None),
            P("dp", "tensor", None),
            P(None, "dp", "tensor"),
            P("tensor", "dp"),
            P("dp", "tensor"),
            P("tensor", "dp"),
            P(None, ("dp", "tensor")),
            P(None, "dp", "tensor"),
            P("tensor", "dp"),
            P("dp", "tensor"),
            P("tensor", "dp"),
            P(None, ("dp", "tensor")),
            P(None, "dp", "tensor"),
            P("tensor", "dp"),
            P("dp", "tensor"),
            P("tensor", "dp"),
            P(None, ("dp", "tensor")),
            P(None, "dp", "tensor"),
            P("tensor", "dp"),
            P("dp", "tensor"),
            P("tensor", "dp"),
            P(None, ("dp", "tensor")),
            P(),
        ),
        check_vma=False,
    )
```

time: 1130 us -> 389 us (0.34)
  waiting for transfers between devices: 490 us -> 78.5 us
  matrix products: 242 us -> 0 us
  blocking collectives: 169 us -> 40.1 us
  Pallas kernels: 0 us -> 125 us
  other arithmetic: 112 us -> 35.6 us
  starting transfers between devices: 0.58 us -> 58.2 us
  local copies, waits for them, and re-layouts: 85.6 us -> 46 us
  between operations: 18 us -> 4.22 us
    dot_general x26 -> x0, matrix products: 242 us -> none  [the longest x2 34.4 us: attend_back(): jnp.einsum('qhd,khd->hqk', grad_heads_row, value_heads, preferred_element...]
    unnamed x15 -> x0, waiting for transfers between devices: 183 us -> none
    reduce_scatter x7 -> x0, waiting for transfers between devices: 183 us -> none  [the longest x1 126 us: shards(): lax.psum_scatter(grad_merge_local, 'dp', scatter_dimension=1, tiled=True)]
    pallas_call x0 -> x10, Pallas kernels: none -> 125 us  [the longest x1 27.7 us: call_attend(): pl.pallas_call(attend_kernel, grid=(PAIRS,), in_specs=[at(0), at(PAIRS),...]
    all_gather x6 -> x0, waiting for transfers between devices: 124 us -> none  [the longest x1 53.3 us: shards(): lax.all_gather(reduce_weight.astype(jnp.bfloat16), 'dp', axis=1, tiled=True)]
    all_gather x2 -> x0, blocking collectives: 88.6 us -> none  [the longest x1 49.1 us: shards(): lax.all_gather(merge_weight.astype(jnp.bfloat16), 'dp', axis=1, tiled=True)]
    ppermute x0 -> x47, waiting for transfers between devices: none -> 78.5 us  [the longest x34 78.5 us: send(): return lax.ppermute(value, ALL, self.perm(where))]
    ppermute x0 -> x47, starting transfers between devices: none -> 58.2 us  [the longest x34 55.4 us: send(): return lax.ppermute(value, ALL, self.perm(where))]
  transfers between devices with their start and end apart: 14 -> 47, of which waited for: 10 -> 16; matrix products, arithmetic and copies ran while one was open for 23% -> 17% of each run, Pallas kernels for 0% -> 32%
where the time goes in v1:
time: 389 us; the launch traced here: 388 us
  Pallas kernels  125 us (32%)
  waiting for transfers between devices  78.5 us (20%)
  starting transfers between devices  58.2 us (15%)
  local copies, waits for them, and re-layouts  46 us (12%)
  blocking collectives  40.1 us (10%)
  other arithmetic  35.6 us (9%)
  between operations  4.22 us (1%)
    ppermute x34, waiting for transfers between devices, send(): return lax.ppermute(value, ALL, self.perm(where))  78.5 us
    ppermute x34, starting transfers between devices, send(): return lax.ppermute(value, ALL, self.perm(where))  55.4 us
    unnamed x1, blocking collectives  40.1 us
    pallas_call x1, Pallas kernels, call_attend(): pl.pallas_call(attend_kernel, grid=(PAIRS,), in_specs=[at(0), at(PAIRS),...  27.7 us
    unnamed x123, local copies, waits for them, and re-layouts  24.8 us
    pallas_call x1, Pallas kernels, call_forward(): pl.pallas_call(forward_kernel, grid=(4,), in_specs=[SMEM, tile, tile, who...  21.8 us
    pallas_call x1, Pallas kernels, call_heads_grad(): pl.pallas_call(heads_grad_kernel, grid=(8,), in_specs=[SMEM, whole((SEQ,...  15.1 us
    pallas_call x1, Pallas kernels, call_attend_back(): pl.pallas_call(attend_back_kernel, grid=(PAIRS,), in_specs=[whole((MARKED...  12 us
  transfers between devices with their start and end apart: 47, of which 16 were waited for; matrix products, arithmetic and copies ran while one was open for 17% of the time, Pallas kernels for 32%

profile of v1, /device:TPU:0, one launch (start us, length us, event | category | flops | bytes accessed | tf_op | source)
XLA Modules:
  0.0 388.0 jit_solution(8309028852364511089)
XLA Ops:
  0.7 1.8 constant_dynamic-update-slice_fusion.4
  2.4 3.0 collective-permute-start
  5.5 2.6 collective-permute-start.1
  9.4 2.4 multiply_reduce_fusion.3
  16.5 3.5 collective-permute-start.8
  30.1 3.8 collective-permute-start.15
  35.1 1.7 collective-permute-start.3
  40.7 1.6 constant_dynamic-update-slice_fusion.8
  42.3 1.6 constant_dynamic-update-slice_fusion.7
  44.6 7.2 %collective-permute-done.10 = bf16[4,48,2048]{2,1,0:T(8,128)(2,1)S(1)} collective-permute-done((bf16[4,48,2048]{2,1,0:T(8,128)(2,1)S(1)}, bf16[4,48,2048]{2,1,0:T(8,128)(2,1)S(1)}, u32[]{:S(2)}, u32[]{:S(2)}) %collective-permute-start.10) | collective-permute-done | bytes 786464 | tf_op jit(solution)/shard_map/ppermute | solution.py:696
  52.8 1.6 collective-permute-start.11
  59.5 11.4 %collective-permute-done.17 = bf16[4,48,1536]{2,1,0:T(8,128)(2,1)S(1)} collective-permute-done((bf16[4,48,1536]{2,1,0:T(8,128)(2,1)S(1)}, bf16[4,48,1536]{2,1,0:T(8,128)(2,1)S(1)}, u32[]{:S(2)}, u32[]{:S(2)}) %collective-permute-start.17) | collective-permute-done | bytes 589856 | tf_op jit(solution)/shard_map/ppermute | solution.py:696
  72.2 14.1 %collective-permute-done.4.b = bf16[8,3,48,384]{3,2,1,0:T(8,128)(2,1)} collective-permute-done((bf16[8,3,48,384]{3,2,1,0:T(8,128)(2,1)}, bf16[8,3,48,384]{3,2,1,0:T(8,128)(2,1)}, u32[]{:S(2)}, u32[]{:S(2)}) %collective-permute-start.4) | collective-permute-done | bytes 884768 | tf_op jit(solution)/shard_map/ppermute | solution.py:696
  93.3 5.7 %collective-permute-done.18.f.b.d = bf16[8,48,1536]{2,1,0:T(8,128)(2,1)} collective-permute-done((bf16[8,48,1536]{2,1,0:T(8,128)(2,1)}, bf16[8,48,1536]{2,1,0:T(8,128)(2,1)}, u32[]{:S(2)}, u32[]{:S(2)}) %collective-permute-start.18) | collective-permute-done | bytes 1179680 | tf_op jit(solution)/shard_map/ppermute | solution.py:696
  99.5 7.4 %project.1.q_ref.k_ref.v_ref = bf16[1024,2304]{1,0:T(8,128)(2,1)S(1)} custom-call(s32[33]{0:T(128)S(1)} %pad_add_fusion.info, bf16[1024,768]{1,0:T(8,128)(2,1)S(1)} %dynamic-slice_bitcast_fusion.1.x_ref, bf16[8,3,48,384]{3,2,1,0:T(8,128)(2,1)} %constant_dynamic-update-slice_fusion.a, bf16[8,3,48,384]{3,2,1,0:T(8,128)(2,1)} %collective-permute-done.4.b, ...), custom_call_target="tpu_custom_call" | custom-call | flops 3623878656 | bytes 10000000 | tf_op jit(solution)/shard_map/project/pallas_call | solution.py:452
  106.9 27.7 %attend.1.ctx_ref = bf16[1024,768]{1,0:T(8,128)(2,1)S(1)} custom-call(bf16[1024,2304]{1,0:T(8,128)(2,1)S(1)} %project.1.q_ref.k_ref.v_ref, bf16[1024,2304]{1,0:T(8,128)(2,1)S(1)} %project.1.q_ref.k_ref.v_ref, bf16[1024,2304]{1,0:T(8,128)(2,1)S(1)} %project.1.q_ref.k_ref.v_ref, s32[1,1024]{1,0:T(1,128)S(1)} %constant_dynamic-slice_fusion.4.seg_row_ref, ...), custom_call_target="tpu_custom_call" | custom-call | flops 4831838208 | bytes 6000000 | tf_op jit(solution)/shard_map/attend/pallas_call | solution.py:469
  141.0 6.9 %marked_one.1 = (bf16[80,768]{1,0:T(8,128)(2,1)S(1)}, bf16[80,768]{1,0:T(8,128)(2,1)S(1)}, f32[80,768]{1,0:T(8,128)S(1)}, f32[80,768]{1,0:T(8,128)S(1)}, bf16[80...) custom-call(s32[33]{0:T(128)S(1)} %pad_add_fusion.info, ...), custom_call_target="tpu_custom_call" | custom-call | flops 1500000000 | bytes 12000000 | tf_op jit(solution)/shard_map/marked_one/pallas_call | solution.py:482
  147.9 7.9 %collective-permute-start.30 = (bf16[80,768]{1,0:T(8,128)(2,1)S(1)}, bf16[80,768]{1,0:T(8,128)(2,1)}, u32[]{:S(2)}, u32[]{:S(2)}) collective-permute-start(bf16[80,768]{1,0:T(8,128)(2,1)S(1)} %get-tuple-element.60), channel_id=1, source_target_pairs={{0,8},{1,9},{2,10},{3,11},{4,12},{5,13},{6,14},{7,15},{8,0},{9,1},... | collective-permute-start | bytes 368648 | tf_op jit(solution)/shard_map/ppermute | solution.py:696
  156.5 2.4 collective-permute-start.32
  158.9 5.8 %marked_two.1 = (f32[80,768]{1,0:T(8,128)S(1)}, bf16[80,768]{1,0:T(8,128)(2,1)S(1)}, f32[2,768]{1,0:T(2,128)S(1)}) custom-call(s32[33]{0:T(128)S(1)} %pad_add_fusion.info, bf16[80,1024]{1,0:T(8,128)(2,1)S(1)} %fusion.2.sel_ref, bf16[512,768]{1,0:T(8,128)(2,1)S(1)} %copy-done.5, bf16[512,768]{1,0:T(8,128)(2,1)} %collective-permute-done.22.cot_b, ...), custom_call_target="tpu_custom_call" | custom-call | flops 1000000000 | bytes 8000000 | tf_op jit(solution)/shard_map/marked_two/pallas_call | solution.py:503
  166.8 9.2 %marked_three.1 = (f32[80,768]{1,0:T(8,128)S(1)}, bf16[80,768]{1,0:T(8,128)(2,1)S(1)}, bf16[80,768]{1,0:T(8,128)(2,1)S(1)}, f32[2,768]{1,0:T(2,128)S(1)}) custom-call(s32[33]{0:T(128)S(1)} %pad_add_fusion.info, f32[4,768]{1,0:T(4,128)S(1)} %reshape.220.norms, f32[80,768]{1,0:T(8,128)S(1)} %get-tuple-element.45.db_ref, ...), custom_call_target="tpu_custom_call" | custom-call | flops 1500000000 | bytes 12000000 | tf_op jit(solution)/shard_map/marked_three/pallas_call | solution.py:520
  176.7 12.0 %attend_back.1 = (bf16[80,768]{1,0:T(8,128)(2,1)S(1)}, bf16[1024,768]{1,0:T(8,128)(2,1)S(1)}, bf16[1024,768]{1,0:T(8,128)(2,1)S(1)}) custom-call(bf16[80,1024]{1,0:T(8,128)(2,1)S(1)} %fusion.2.sel_ref, bf16[1024,2304]{1,0:T(8,128)(2,1)S(1)} %bitcast.102, bf16[1024,2304]{1,0:T(8,128)(2,1)S(1)} %bitcast.102, bf16[1024,2304]{1,0:T(8,128)(2,1)S(1)} %bitcast.102, ...), custom_call_target="tpu_custom_call" | custom-call | flops 1509949440 | bytes 8000000 | tf_op jit(solution)/shard_map/attend_back/pallas_call | solution.py:550
  188.7 8.1 %input_grad.1 = f32[1024,768]{1,0:T(8,128)S(1)} custom-call(s32[33]{0:T(128)S(1)} %pad_add_fusion.info, bf16[1024,768]{1,0:T(8,128)(2,1)S(1)} %get-tuple-element.50.dk_ref, bf16[1024,768]{1,0:T(8,128)(2,1)S(1)} %get-tuple-element.51.dv_ref, bf16[80,1024]{1,0:T(8,128)(2,1)S(1)} %fusion.2.sel_ref, f32[80,768]{1,0:T(8,128)S(1)} %get-tuple-element.52.da_ref, ...), custom_call_target="tpu_custom_call" | custom-call | flops 2415919104 | bytes 10000000 | tf_op jit(solution)/shard_map/input_grad/pallas_call | solution.py:624
  199.1 40.1 %all-reduce.1 = f32[4,768]{1,0:T(4,128)S(1)} all-reduce(f32[4,768]{1,0:T(4,128)S(1)} %pad_maximum_fusion.8), channel_id=2, replica_groups=mesh['dp'=16,'tensor'=2] {'dp','tensor'}, use_global_device_ids=true, to_apply=%region_5.6.clone | all-reduce | flops 3072 | bytes 24576
  242.9 15.1 %heads_grad.1 = (bf16[8,48,1536]{2,1,0:T(8,128)(2,1)S(1)}, bf16[8,48,1536]{2,1,0:T(8,128)(2,1)S(1)}, bf16[16,48,1536]{2,1,0:T(8,128)(2,1)S(1)}) custom-call(s32[33]{0:T(128)S(1)} %pad_add_fusion.info, bf16[1024,768]{1,0:T(8,128)(2,1)S(1)} %copy-done.4, bf16[1024,768]{1,0:T(8,128)(2,1)S(1)} %copy-done.9, bf16[1024,768]{1,0:T(8,128)(2,1)S(1)} %copy-done.11, ...), custom_call_target="tpu_custom_call" | custom-call | flops 2415919104 | bytes 12000000 | tf_op jit(solution)/shard_map/heads_grad/pallas_call | solution.py:574
  258.8 21.8 %forward_rest.1 = bf16[1024,768]{1,0:T(8,128)(2,1)} custom-call(s32[33]{0:T(128)S(1)} %pad_add_fusion.info, bf16[1024,768]{1,0:T(8,128)(2,1)} %copy-done.3, bf16[1024,768]{1,0:T(8,128)(2,1)} %copy-done.6, f32[4,768]{1,0:T(4,128)S(1)} %reshape.220.norms, bf16[8,48,2048]{2,1,0:T(8,128)(2,1)} %constant_dynamic-update-slice_fusion.5.a, ...), custom_call_target="tpu_custom_call" | custom-call | flops 10871635968 | bytes 14000000 | tf_op jit(solution)/shard_map/forward_rest/pallas_call | solution.py:655
  280.6 2.4 dynamic-slice_bitcast_fusion.4
  283.1 2.3 collective-permute-start.36
  287.6 2.3 collective-permute-done.36
  296.1 11.4 %ffn_grad.1 = bf16[4,48,3072]{2,1,0:T(8,128)(2,1)S(1)} custom-call(s32[33]{0:T(128)S(1)} %pad_add_fusion.info, bf16[640,768]{1,0:T(8,128)(2,1)S(1)} %constant_dynamic-update-slice_fusion.15.yb_ref, bf16[640,768]{1,0:T(8,128)(2,1)S(1)} %constant_dynamic-update-slice_fusion.20.db_ref, bf16[640,192]{1,0:T(8,128)(2,1)S(1)} %constant_dynamic-slice_fusion.1.ybc_ref, ...), custom_call_target="tpu_custom_call" | custom-call | flops 5000000000 | bytes 10000000 | tf_op jit(solution)/shard_map/ffn_grad/pallas_call | solution.py:602
  307.5 2.2 collective-permute-start.38
  309.9 1.9 maximum_select_fusion
  313.3 4.3 %collective-permute-done.38 = bf16[2,48,3072]{2,1,0:T(8,128)(2,1)S(1)} collective-permute-done((bf16[2,48,3072]{2,1,0:T(8,128)(2,1)S(1)}, bf16[2,48,3072]{2,1,0:T(8,128)(2,1)S(1)}, u32[]{:S(2)}, u32[]{:S(2)}) %collective-permute-start.38) | collective-permute-done | bytes 589856 | tf_op jit(solution)/shard_map/ppermute | solution.py:696
  317.8 2.1 collective-permute-start.39
  319.9 13.5 %collective-permute-done.25 = bf16[8,48,1536]{2,1,0:T(8,128)(2,1)S(1)} collective-permute-done((bf16[8,48,1536]{2,1,0:T(8,128)(2,1)S(1)}, bf16[8,48,1536]{2,1,0:T(8,128)(2,1)S(1)}, u32[]{:S(2)}, u32[]{:S(2)}) %collective-permute-start.25) | collective-permute-done | bytes 1179680 | tf_op jit(solution)/shard_map/ppermute | solution.py:696
  334.0 2.1 collective-permute-start.26
  336.1 1.7 multiply_reduce_fusion.1
  337.8 6.1 %collective-permute-done.26 = bf16[4,48,1536]{2,1,0:T(8,128)(2,1)S(1)} collective-permute-done((bf16[4,48,1536]{2,1,0:T(8,128)(2,1)S(1)}, bf16[4,48,1536]{2,1,0:T(8,128)(2,1)S(1)}, u32[]{:S(2)}, u32[]{:S(2)}) %collective-permute-start.26) | collective-permute-done | bytes 589856 | tf_op jit(solution)/shard_map/ppermute | solution.py:696
  344.2 2.3 collective-permute-start.29
  346.7 2.0 collective-permute-start.27
  348.6 1.7 multiply_reduce_fusion
  350.4 2.5 collective-permute-done.29
  352.9 5.9 %collective-permute-done.28 = bf16[48,1536]{1,0:T(8,128)(2,1)S(1)} collective-permute-done((bf16[48,1536]{1,0:T(8,128)(2,1)S(1)}, bf16[48,1536]{1,0:T(8,128)(2,1)S(1)}, u32[]{:S(2)}, u32[]{:S(2)}) %collective-permute-start.28) | collective-permute-done | bytes 147488 | tf_op jit(solution)/shard_map/ppermute | solution.py:696
  361.3 2.0 concatenate.76
  363.3 1.9 concatenate.75
  365.4 3.4 maximum_select_fusion.1
  368.8 2.2 collective-permute-start.43
  375.3 2.3 collective-permute-start.46
  (274 shorter events, 78.5 us)
Async XLA Ops:
  0.7 88.5 %copy-start = (bf16[2,1024,768]{2,1,0:T(8,128)(2,1)S(1)}, bf16[2,1024,768]{2,1,0:T(8,128)(2,1)}, u32[]{:S(2)}) copy-start(bf16[2,1024,768]{2,1,0:T(8,128)(2,1)} %param.20) | copy-start | bytes 9437188
  2.4 23.9 %collective-permute-start = (bf16[1,3,48,384]{3,2,1,0:T(8,128)(2,1)S(1)}, bf16[1,3,48,384]{3,2,1,0:T(8,128)(2,1)}, u32[]{:S(2)}, u32[]{:S(2)}) collective-permute-start(bf16[1,3,48,384]{3,2,1,0:T(8,128)(2,1)S(1)} %get-tuple-element.95), channel_id=1, source_target_pairs={{0,8},{1,9},{2,10},{3,11},{4,12},{5,13},{6,14},{7,15},{8,0},{9,1},... | collective-permute-start | bytes 331784 | tf_op jit(solution)/shard_map/ppermute | solution.py:696
  5.5 22.5 %collective-permute-start.1 = (bf16[1,3,48,384]{3,2,1,0:T(8,128)(2,1)S(1)}, bf16[1,3,48,384]{3,2,1,0:T(8,128)(2,1)}, u32[]{:S(2)}, u32[]{:S(2)}) collective-permute-start(bf16[1,3,48,384]{3,2,1,0:T(8,128)(2,1)S(1)} %get-tuple-element.95), channel_id=1, source_target_pairs={{0,16},{1,17},{2,18},{3,19},{4,20},{5,21},{6,22},{7,23},{8,24},{9,... | collective-permute-start | bytes 331784 | tf_op jit(solution)/shard_map/ppermute | solution.py:696
  8.1 22.0 %collective-permute-start.2 = (bf16[1,3,48,384]{3,2,1,0:T(8,128)(2,1)S(1)}, bf16[1,3,48,384]{3,2,1,0:T(8,128)(2,1)}, u32[]{:S(2)}, u32[]{:S(2)}) collective-permute-start(bf16[1,3,48,384]{3,2,1,0:T(8,128)(2,1)S(1)} %get-tuple-element.95), channel_id=1, source_target_pairs={{0,24},{1,25},{2,26},{3,27},{4,28},{5,29},{6,30},{7,31},{8,16},{9,... | collective-permute-start | bytes 331784 | tf_op jit(solution)/shard_map/ppermute | solution.py:696
  15.6 19.4 %collective-permute-start.7 = (bf16[1,48,2048]{2,1,0:T(8,128)(2,1)}, bf16[1,48,2048]{2,1,0:T(8,128)(2,1)}, u32[]{:S(2)}, u32[]{:S(2)}) collective-permute-start(bf16[1,48,2048]{2,1,0:T(8,128)(2,1)} %maximum_bitcast_fusion), channel_id=1, source_target_pairs={{0,8},{1,9},{2,10},{3,11},{4,12},{5,13},{6,14},{7,15},{8,0},{9,1},... | collective-permute-start | bytes 589832 | tf_op jit(solution)/shard_map/ppermute | solution.py:696
  16.5 18.5 %collective-permute-start.8 = (bf16[1,48,2048]{2,1,0:T(8,128)(2,1)}, bf16[1,48,2048]{2,1,0:T(8,128)(2,1)}, u32[]{:S(2)}, u32[]{:S(2)}) collective-permute-start(bf16[1,48,2048]{2,1,0:T(8,128)(2,1)} %maximum_bitcast_fusion), channel_id=1, source_target_pairs={{0,16},{1,17},{2,18},{3,19},{4,20},{5,21},{6,22},{7,23},{8,24},{9,... | collective-permute-start | bytes 589832 | tf_op jit(solution)/shard_map/ppermute | solution.py:696
  26.3 10.5 %collective-permute-start.9 = (bf16[1,48,2048]{2,1,0:T(8,128)(2,1)}, bf16[1,48,2048]{2,1,0:T(8,128)(2,1)S(1)}, u32[]{:S(2)}, u32[]{:S(2)}) collective-permute-start(bf16[1,48,2048]{2,1,0:T(8,128)(2,1)} %maximum_bitcast_fusion), channel_id=1, source_target_pairs={{0,24},{1,25},{2,26},{3,27},{4,28},{5,29},{6,30},{7,31},{8,16},{9,... | collective-permute-start | bytes 589832 | tf_op jit(solution)/shard_map/ppermute | solution.py:696
  28.0 26.5 %collective-permute-start.14 = (bf16[1,48,1536]{2,1,0:T(8,128)(2,1)}, bf16[1,48,1536]{2,1,0:T(8,128)(2,1)S(1)}, u32[]{:S(2)}, u32[]{:S(2)}) collective-permute-start(bf16[1,48,1536]{2,1,0:T(8,128)(2,1)} %get-tuple-element.93), channel_id=1, source_target_pairs={{0,8},{1,9},{2,10},{3,11},{4,12},{5,13},{6,14},{7,15},{8,0},{9,1},... | collective-permute-start | bytes 442376 | tf_op jit(solution)/shard_map/ppermute | solution.py:696
  30.1 24.4 %collective-permute-start.15 = (bf16[1,48,1536]{2,1,0:T(8,128)(2,1)}, bf16[1,48,1536]{2,1,0:T(8,128)(2,1)S(1)}, u32[]{:S(2)}, u32[]{:S(2)}) collective-permute-start(bf16[1,48,1536]{2,1,0:T(8,128)(2,1)} %get-tuple-element.93), channel_id=1, source_target_pairs={{0,16},{1,17},{2,18},{3,19},{4,20},{5,21},{6,22},{7,23},{8,24},{9,... | collective-permute-start | bytes 442376 | tf_op jit(solution)/shard_map/ppermute | solution.py:696
  35.0 19.5 %collective-permute-start.16 = (bf16[1,48,1536]{2,1,0:T(8,128)(2,1)}, bf16[1,48,1536]{2,1,0:T(8,128)(2,1)S(1)}, u32[]{:S(2)}, u32[]{:S(2)}) collective-permute-start(bf16[1,48,1536]{2,1,0:T(8,128)(2,1)} %get-tuple-element.93), channel_id=1, source_target_pairs={{0,24},{1,25},{2,26},{3,27},{4,28},{5,29},{6,30},{7,31},{8,16},{9,... | collective-permute-start | bytes 442376 | tf_op jit(solution)/shard_map/ppermute | solution.py:696
  35.1 21.8 %collective-permute-start.3 = (bf16[4,3,48,384]{3,2,1,0:T(8,128)(2,1)S(1)}, bf16[4,3,48,384]{3,2,1,0:T(8,128)(2,1)S(1)}, u32[]{:S(2)}, u32[]{:S(2)}) collective-permute-start(bf16[4,3,48,384]{3,2,1,0:T(8,128)(2,1)S(1)} %pad_maximum_fusion.4), channel_id=1, source_target_pairs={{0,4},{1,3},{2,6},{3,1},{4,0},{5,7},{6,2},{7,5},{8,12},{9,11},{10,... | collective-permute-start | bytes 1327112 | tf_op jit(solution)/shard_map/ppermute | solution.py:696
  38.0 13.8 %collective-permute-start.10 = (bf16[4,48,2048]{2,1,0:T(8,128)(2,1)S(1)}, bf16[4,48,2048]{2,1,0:T(8,128)(2,1)S(1)}, u32[]{:S(2)}, u32[]{:S(2)}) collective-permute-start(bf16[4,48,2048]{2,1,0:T(8,128)(2,1)S(1)} %pad_maximum_fusion), channel_id=1, source_target_pairs={{0,4},{1,3},{2,6},{3,1},{4,0},{5,7},{6,2},{7,5},{8,12},{9,11},{10,... | collective-permute-start | bytes 2359304 | tf_op jit(solution)/shard_map/ppermute | solution.py:696
  52.8 34.3 %collective-permute-start.11 = (bf16[8,48,2048]{2,1,0:T(8,128)(2,1)}, bf16[8,48,2048]{2,1,0:T(8,128)(2,1)}, u32[]{:S(2)}, u32[]{:S(2)}) collective-permute-start(bf16[8,48,2048]{2,1,0:T(8,128)(2,1)} %constant_dynamic-update-slice_fusion.5.a), channel_id=1, source_target_pairs={{0,2},{1,5},{2,0},{3,7},{4,6},{5,1},{6,4},{7,3},{8,10},{9,13},{10,... | collective-permute-start | bytes 4718600 | tf_op jit(solution)/shard_map/ppermute | solution.py:696
  54.6 16.3 %collective-permute-start.17 = (bf16[4,48,1536]{2,1,0:T(8,128)(2,1)S(1)}, bf16[4,48,1536]{2,1,0:T(8,128)(2,1)S(1)}, u32[]{:S(2)}, u32[]{:S(2)}) collective-permute-start(bf16[4,48,1536]{2,1,0:T(8,128)(2,1)S(1)} %pad_maximum_fusion.1), channel_id=1, source_target_pairs={{0,4},{1,3},{2,6},{3,1},{4,0},{5,7},{6,2},{7,5},{8,12},{9,11},{10,... | collective-permute-start | bytes 1769480 | tf_op jit(solution)/shard_map/ppermute | solution.py:696
  57.6 28.7 %collective-permute-start.4 = (bf16[8,3,48,384]{3,2,1,0:T(8,128)(2,1)}, bf16[8,3,48,384]{3,2,1,0:T(8,128)(2,1)}, u32[]{:S(2)}, u32[]{:S(2)}) collective-permute-start(bf16[8,3,48,384]{3,2,1,0:T(8,128)(2,1)} %constant_dynamic-update-slice_fusion.a), channel_id=1, source_target_pairs={{0,2},{1,5},{2,0},{3,7},{4,6},{5,1},{6,4},{7,3},{8,10},{9,13},{10,... | collective-permute-start | bytes 2654216 | tf_op jit(solution)/shard_map/ppermute | solution.py:696
  71.8 27.2 %collective-permute-start.18 = (bf16[8,48,1536]{2,1,0:T(8,128)(2,1)}, bf16[8,48,1536]{2,1,0:T(8,128)(2,1)}, u32[]{:S(2)}, u32[]{:S(2)}) collective-permute-start(bf16[8,48,1536]{2,1,0:T(8,128)(2,1)} %constant_dynamic-update-slice_fusion.10.e.a.c), channel_id=1, source_target_pairs={{0,2},{1,5},{2,0},{3,7},{4,6},{5,1},{6,4},{7,3},{8,10},{9,13},{10,... | collective-permute-start | bytes 3538952 | tf_op jit(solution)/shard_map/ppermute | solution.py:696
  72.2 20.6 %collective-permute-start.5 = (bf16[8,3,48,384]{3,2,1,0:T(8,128)(2,1)}, bf16[8,3,48,384]{3,2,1,0:T(8,128)(2,1)}, u32[]{:S(2)}, u32[]{:S(2)}) collective-permute-start(bf16[8,3,48,384]{3,2,1,0:T(8,128)(2,1)} %constant_dynamic-update-slice_fusion.a), channel_id=1, source_target_pairs={{0,1},{1,0},{2,3},{3,2},{4,5},{5,4},{6,7},{7,6},{8,9},{9,8},{10,11... | collective-permute-start | bytes 2654216 | tf_op jit(solution)/shard_map/ppermute | solution.py:717
  86.4 12.6 %collective-permute-start.6 = (bf16[8,3,48,384]{3,2,1,0:T(8,128)(2,1)}, bf16[8,3,48,384]{3,2,1,0:T(8,128)(2,1)}, u32[]{:S(2)}, u32[]{:S(2)}) collective-permute-start(bf16[8,3,48,384]{3,2,1,0:T(8,128)(2,1)} %collective-permute-done.4.b), channel_id=1, source_target_pairs={{0,1},{1,0},{2,3},{3,2},{4,5},{5,4},{6,7},{7,6},{8,9},{9,8},{10,11... | collective-permute-start | bytes 2654216 | tf_op jit(solution)/shard_map/ppermute | solution.py:717
  86.5 50.6 %collective-permute-start.12 = (bf16[8,48,2048]{2,1,0:T(8,128)(2,1)}, bf16[8,48,2048]{2,1,0:T(8,128)(2,1)}, u32[]{:S(2)}, u32[]{:S(2)}) collective-permute-start(bf16[8,48,2048]{2,1,0:T(8,128)(2,1)} %constant_dynamic-update-slice_fusion.5.a), channel_id=1, source_target_pairs={{0,1},{1,0},{2,3},{3,2},{4,5},{5,4},{6,7},{7,6},{8,9},{9,8},{10,11... | collective-permute-start | bytes 4718600 | tf_op jit(solution)/shard_map/ppermute | solution.py:717
  87.1 50.8 %collective-permute-start.13 = (bf16[8,48,2048]{2,1,0:T(8,128)(2,1)}, bf16[8,48,2048]{2,1,0:T(8,128)(2,1)}, u32[]{:S(2)}, u32[]{:S(2)}) collective-permute-start(bf16[8,48,2048]{2,1,0:T(8,128)(2,1)} %collective-permute-done.11.b), channel_id=1, source_target_pairs={{0,1},{1,0},{2,3},{3,2},{4,5},{5,4},{6,7},{7,6},{8,9},{9,8},{10,11... | collective-permute-start | bytes 4718600 | tf_op jit(solution)/shard_map/ppermute | solution.py:717
  92.8 63.6 %collective-permute-start.22 = (bf16[512,768]{1,0:T(8,128)(2,1)}, bf16[512,768]{1,0:T(8,128)(2,1)}, u32[]{:S(2)}, u32[]{:S(2)}) collective-permute-start(bf16[512,768]{1,0:T(8,128)(2,1)} %get-tuple-element.96), channel_id=1, source_target_pairs={{0,1},{1,0},{2,3},{3,2},{4,5},{5,4},{6,7},{7,6},{8,9},{9,8},{10,11... | collective-permute-start | bytes 2359304 | tf_op jit(solution)/shard_map/ppermute | solution.py:717
  99.0 59.9 %collective-permute-start.19 = (bf16[8,48,1536]{2,1,0:T(8,128)(2,1)}, bf16[8,48,1536]{2,1,0:T(8,128)(2,1)S(1)}, u32[]{:S(2)}, u32[]{:S(2)}) collective-permute-start(bf16[8,48,1536]{2,1,0:T(8,128)(2,1)} %constant_dynamic-update-slice_fusion.10.e.a.c), channel_id=1, source_target_pairs={{0,1},{1,0},{2,3},{3,2},{4,5},{5,4},{6,7},{7,6},{8,9},{9,8},{10,11... | collective-permute-start | bytes 3538952 | tf_op jit(solution)/shard_map/ppermute | solution.py:717
  99.0 59.9 %collective-permute-start.20 = (bf16[8,48,1536]{2,1,0:T(8,128)(2,1)}, bf16[8,48,1536]{2,1,0:T(8,128)(2,1)}, u32[]{:S(2)}, u32[]{:S(2)}) collective-permute-start(bf16[8,48,1536]{2,1,0:T(8,128)(2,1)} %collective-permute-done.18.f.b.d), channel_id=1, source_target_pairs={{0,1},{1,0},{2,3},{3,2},{4,5},{5,4},{6,7},{7,6},{8,9},{9,8},{10,11... | collective-permute-start | bytes 3538952 | tf_op jit(solution)/shard_map/ppermute | solution.py:717
  147.9 135.1 %collective-permute-start.30 = (bf16[80,768]{1,0:T(8,128)(2,1)S(1)}, bf16[80,768]{1,0:T(8,128)(2,1)}, u32[]{:S(2)}, u32[]{:S(2)}) collective-permute-start(bf16[80,768]{1,0:T(8,128)(2,1)S(1)} %get-tuple-element.60), channel_id=1, source_target_pairs={{0,8},{1,9},{2,10},{3,11},{4,12},{5,13},{6,14},{7,15},{8,0},{9,1},... | collective-permute-start | bytes 368648 | tf_op jit(solution)/shard_map/ppermute | solution.py:696
  155.8 129.6 %collective-permute-start.31 = (bf16[80,768]{1,0:T(8,128)(2,1)S(1)}, bf16[80,768]{1,0:T(8,128)(2,1)}, u32[]{:S(2)}, u32[]{:S(2)}) collective-permute-start(bf16[80,768]{1,0:T(8,128)(2,1)S(1)} %get-tuple-element.60), channel_id=1, source_target_pairs={{0,16},{1,17},{2,18},{3,19},{4,20},{5,21},{6,22},{7,23},{8,24},{9,... | collective-permute-start | bytes 368648 | tf_op jit(solution)/shard_map/ppermute | solution.py:696
  156.5 129.0 %collective-permute-start.32 = (bf16[80,768]{1,0:T(8,128)(2,1)S(1)}, bf16[80,768]{1,0:T(8,128)(2,1)}, u32[]{:S(2)}, u32[]{:S(2)}) collective-permute-start(bf16[80,768]{1,0:T(8,128)(2,1)S(1)} %get-tuple-element.60), channel_id=1, source_target_pairs={{0,24},{1,25},{2,26},{3,27},{4,28},{5,29},{6,30},{7,31},{8,16},{9,... | collective-permute-start | bytes 368648 | tf_op jit(solution)/shard_map/ppermute | solution.py:696
  164.8 122.2 %collective-permute-start.34 = (bf16[80,768]{1,0:T(8,128)(2,1)S(1)}, bf16[80,768]{1,0:T(8,128)(2,1)}, u32[]{:S(2)}, u32[]{:S(2)}) collective-permute-start(bf16[80,768]{1,0:T(8,128)(2,1)S(1)} %get-tuple-element.46.dbb_ref), channel_id=1, source_target_pairs={{0,8},{1,9},{2,10},{3,11},{4,12},{5,13},{6,14},{7,15},{8,0},{9,1},... | collective-permute-start | bytes 368648 | tf_op jit(solution)/shard_map/ppermute | solution.py:696
  165.9 121.3 %collective-permute-start.35 = (bf16[80,768]{1,0:T(8,128)(2,1)S(1)}, bf16[80,768]{1,0:T(8,128)(2,1)}, u32[]{:S(2)}, u32[]{:S(2)}) collective-permute-start(bf16[80,768]{1,0:T(8,128)(2,1)S(1)} %get-tuple-element.46.dbb_ref), channel_id=1, source_target_pairs={{0,16},{1,17},{2,18},{3,19},{4,20},{5,21},{6,22},{7,23},{8,24},{9,... | collective-permute-start | bytes 368648 | tf_op jit(solution)/shard_map/ppermute | solution.py:696
  283.1 6.9 %collective-permute-start.36 = (bf16[80,768]{1,0:T(8,128)(2,1)S(1)}, bf16[80,768]{1,0:T(8,128)(2,1)S(1)}, u32[]{:S(2)}, u32[]{:S(2)}) collective-permute-start(bf16[80,768]{1,0:T(8,128)(2,1)S(1)} %get-tuple-element.46.dbb_ref), channel_id=1, source_target_pairs={{0,24},{1,25},{2,26},{3,27},{4,28},{5,29},{6,30},{7,31},{8,16},{9,... | collective-permute-start | bytes 368648 | tf_op jit(solution)/shard_map/ppermute | solution.py:696
  285.4 79.9 %collective-permute-start.21 = (bf16[512,768]{1,0:T(8,128)(2,1)S(1)}, bf16[512,768]{1,0:T(8,128)(2,1)}, u32[]{:S(2)}, u32[]{:S(2)}) collective-permute-start(bf16[512,768]{1,0:T(8,128)(2,1)S(1)} %get-tuple-element.99), channel_id=1, source_target_pairs={{0,1},{1,0},{2,3},{3,2},{4,5},{5,4},{6,7},{7,6},{8,9},{9,8},{10,11... | collective-permute-start | bytes 2359304 | tf_op jit(solution)/shard_map/ppermute | solution.py:717
  285.4 26.3 %collective-permute-start.24 = (bf16[16,48,1536]{2,1,0:T(8,128)(2,1)S(1)}, bf16[16,48,1536]{2,1,0:T(8,128)(2,1)S(1)}, u32[]{:S(2)}, u32[]{:S(2)}) collective-permute-start(bf16[16,48,1536]{2,1,0:T(8,128)(2,1)S(1)} %get-tuple-element.58), channel_id=1, source_target_pairs={{0,1},{1,0},{2,3},{3,2},{4,5},{5,4},{6,7},{7,6},{8,9},{9,8},{10,11... | collective-permute-start | bytes 7077896 | tf_op jit(solution)/shard_map/ppermute | solution.py:717
  287.0 22.7 %collective-permute-start.23 = (bf16[512,768]{1,0:T(8,128)(2,1)S(1)}, bf16[512,768]{1,0:T(8,128)(2,1)S(1)}, u32[]{:S(2)}, u32[]{:S(2)}) collective-permute-start(bf16[512,768]{1,0:T(8,128)(2,1)S(1)} %copy-done.29), channel_id=1, source_target_pairs={{0,1},{1,0},{2,3},{3,2},{4,5},{5,4},{6,7},{7,6},{8,9},{9,8},{10,11... | collective-permute-start | bytes 2359304 | tf_op jit(solution)/shard_map/ppermute | solution.py:717
  287.2 8.4 %collective-permute-start.33 = (bf16[320,768]{1,0:T(8,128)(2,1)S(1)}, bf16[320,768]{1,0:T(8,128)(2,1)S(1)}, u32[]{:S(2)}, u32[]{:S(2)}) collective-permute-start(bf16[320,768]{1,0:T(8,128)(2,1)S(1)} %pad_maximum_fusion.2), channel_id=1, source_target_pairs={{0,1},{1,0},{2,3},{3,2},{4,5},{5,4},{6,7},{7,6},{8,9},{9,8},{10,11... | collective-permute-start | bytes 1474568 | tf_op jit(solution)/shard_map/ppermute | solution.py:717
  290.9 4.9 %collective-permute-start.37 = (bf16[320,768]{1,0:T(8,128)(2,1)S(1)}, bf16[320,768]{1,0:T(8,128)(2,1)S(1)}, u32[]{:S(2)}, u32[]{:S(2)}) collective-permute-start(bf16[320,768]{1,0:T(8,128)(2,1)S(1)} %pad_maximum_fusion.3), channel_id=1, source_target_pairs={{0,1},{1,0},{2,3},{3,2},{4,5},{5,4},{6,7},{7,6},{8,9},{9,8},{10,11... | collective-permute-start | bytes 1474568 | tf_op jit(solution)/shard_map/ppermute | solution.py:717
  307.5 10.1 %collective-permute-start.38 = (bf16[2,48,3072]{2,1,0:T(8,128)(2,1)S(1)}, bf16[2,48,3072]{2,1,0:T(8,128)(2,1)S(1)}, u32[]{:S(2)}, u32[]{:S(2)}) collective-permute-start(bf16[2,48,3072]{2,1,0:T(8,128)(2,1)S(1)} %slice.178), channel_id=1, source_target_pairs={{0,2},{1,5},{2,0},{3,7},{4,6},{5,1},{6,4},{7,3},{8,10},{9,13},{10,... | collective-permute-start | bytes 1769480 | tf_op jit(solution)/shard_map/ppermute | solution.py:696
  312.1 21.3 %collective-permute-start.25 = (bf16[8,48,1536]{2,1,0:T(8,128)(2,1)S(1)}, bf16[8,48,1536]{2,1,0:T(8,128)(2,1)S(1)}, u32[]{:S(2)}, u32[]{:S(2)}) collective-permute-start(bf16[8,48,1536]{2,1,0:T(8,128)(2,1)S(1)} %add_convert_fusion), channel_id=1, source_target_pairs={{0,2},{1,5},{2,0},{3,7},{4,6},{5,1},{6,4},{7,3},{8,10},{9,13},{10,... | collective-permute-start | bytes 3538952 | tf_op jit(solution)/shard_map/ppermute | solution.py:696
  317.8 18.2 %collective-permute-start.39 = (bf16[48,3072]{1,0:T(8,128)(2,1)S(1)}, bf16[48,3072]{1,0:T(8,128)(2,1)S(1)}, u32[]{:S(2)}, u32[]{:S(2)}) collective-permute-start(bf16[48,3072]{1,0:T(8,128)(2,1)S(1)} %fusion.5), channel_id=1, source_target_pairs={{0,4},{1,3},{2,6},{3,1},{4,0},{5,7},{6,2},{7,5},{8,12},{9,11},{10,... | collective-permute-start | bytes 884744 | tf_op jit(solution)/shard_map/ppermute | solution.py:696
  334.0 10.0 %collective-permute-start.26 = (bf16[4,48,1536]{2,1,0:T(8,128)(2,1)S(1)}, bf16[4,48,1536]{2,1,0:T(8,128)(2,1)S(1)}, u32[]{:S(2)}, u32[]{:S(2)}) collective-permute-start(bf16[4,48,1536]{2,1,0:T(8,128)(2,1)S(1)} %slice.214), channel_id=1, source_target_pairs={{0,4},{1,3},{2,6},{3,1},{4,0},{5,7},{6,2},{7,5},{8,12},{9,11},{10,... | collective-permute-start | bytes 1769480 | tf_op jit(solution)/shard_map/ppermute | solution.py:696
  344.2 8.7 %collective-permute-start.29 = (bf16[48,1536]{1,0:T(8,128)(2,1)S(1)}, bf16[48,1536]{1,0:T(8,128)(2,1)S(1)}, u32[]{:S(2)}, u32[]{:S(2)}) collective-permute-start(bf16[48,1536]{1,0:T(8,128)(2,1)S(1)} %get-tuple-element.101), channel_id=1, source_target_pairs={{0,24},{1,25},{2,26},{3,27},{4,28},{5,29},{6,30},{7,31},{8,16},{9,... | collective-permute-start | bytes 442376 | tf_op jit(solution)/shard_map/ppermute | solution.py:696
  346.5 12.2 %collective-permute-start.28 = (bf16[48,1536]{1,0:T(8,128)(2,1)S(1)}, bf16[48,1536]{1,0:T(8,128)(2,1)S(1)}, u32[]{:S(2)}, u32[]{:S(2)}) collective-permute-start(bf16[48,1536]{1,0:T(8,128)(2,1)S(1)} %get-tuple-element.102), channel_id=1, source_target_pairs={{0,16},{1,17},{2,18},{3,19},{4,20},{5,21},{6,22},{7,23},{8,24},{9,... | collective-permute-start | bytes 442376 | tf_op jit(solution)/shard_map/ppermute | solution.py:696
  346.7 12.1 %collective-permute-start.27 = (bf16[48,1536]{1,0:T(8,128)(2,1)S(1)}, bf16[48,1536]{1,0:T(8,128)(2,1)S(1)}, u32[]{:S(2)}, u32[]{:S(2)}) collective-permute-start(bf16[48,1536]{1,0:T(8,128)(2,1)S(1)} %get-tuple-element.100), channel_id=1, source_target_pairs={{0,8},{1,9},{2,10},{3,11},{4,12},{5,13},{6,14},{7,15},{8,0},{9,1},... | collective-permute-start | bytes 442376 | tf_op jit(solution)/shard_map/ppermute | solution.py:696
  365.2 3.6 collective-permute-start.40
  368.8 4.5 %collective-permute-start.43 = (f32[2,10]{1,0:T(2,128)S(1)}, f32[2,10]{1,0:T(2,128)S(1)}, u32[]{:S(2)}, u32[]{:S(2)}) collective-permute-start(f32[2,10]{1,0:T(2,128)S(1)} %fusion.39), channel_id=1, source_target_pairs={{0,6},{1,7},{2,4},{3,5},{4,2},{5,3},{6,0},{7,1},{8,14},{9,15},{10,... | collective-permute-start | bytes 248 | tf_op jit(solution)/shard_map/ppermute | solution.py:696
  371.0 3.6 collective-permute-start.42
  371.7 3.6 collective-permute-start.41
  375.2 4.5 %collective-permute-start.45 = (f32[2,10]{1,0:T(2,128)S(1)}, f32[2,10]{1,0:T(2,128)S(1)}, u32[]{:S(2)}, u32[]{:S(2)}) collective-permute-start(f32[2,10]{1,0:T(2,128)S(1)} %add_add_fusion.1), channel_id=1, source_target_pairs={{0,16},{1,17},{2,18},{3,19},{4,20},{5,21},{6,22},{7,23},{8,24},{9,... | collective-permute-start | bytes 248 | tf_op jit(solution)/shard_map/ppermute | solution.py:696
  375.3 5.4 %collective-permute-start.46 = (f32[2,10]{1,0:T(2,128)S(1)}, f32[2,10]{1,0:T(2,128)S(1)}, u32[]{:S(2)}, u32[]{:S(2)}) collective-permute-start(f32[2,10]{1,0:T(2,128)S(1)} %add_add_fusion.1), channel_id=1, source_target_pairs={{0,24},{1,25},{2,26},{3,27},{4,28},{5,29},{6,30},{7,31},{8,16},{9,... | collective-permute-start | bytes 248 | tf_op jit(solution)/shard_map/ppermute | solution.py:696
  377.7 3.6 collective-permute-start.44
  (52 other events, 639.1 us)
